TPU v7x, 32 devices: a whole 2x2x4 slice. The times are simulated.
32 devices in a mesh: replica: 8 (over y, x, core), shard: 4 (over z).
Axes of the slice: x: 2, y: 2, z: 4, core: 2. Of those that a mesh axis runs over, the one named last changes fastest.
Arguments:
- inputs: bfloat16 [8, 1024, 1024], P('replica', 'shard'), may hold values from -6 to 6
- out_grad: bfloat16 [8, 1024, 1024], P('replica', 'shard'), may hold values from -6 to 6
- segment_ids: int32 [8, 1024], P('replica'), may hold values from 0 to 2, never falling along the last dimension, each value on 1 to 512 neighbouring positions
- ln_gain_attn: bfloat16 [1024], P('shard'), may hold values from 0.5 to 1.5
- ln_bias_attn: bfloat16 [1024], P('shard'), may hold values from -3 to 3
- ln_gain_mlp: bfloat16 [1024], P('shard'), may hold values from 0.5 to 1.5
- ln_bias_mlp: bfloat16 [1024], P('shard'), may hold values from -3 to 3
- qkv_weight: bfloat16 [1024, 3072], P('shard'), may hold values from -0.1875 to 0.1875
- qkv_bias: bfloat16 [3072], P('shard'), may hold values from -3 to 3
- out_weight: bfloat16 [1024, 1024], P('shard'), may hold values from -0.75 to 0.75
- up_weight: bfloat16 [1024, 4096], P('shard'), may hold values from -0.1875 to 0.1875
- up_bias: bfloat16 [4096], P('shard'), may hold values from -3 to 3
- down_weight: bfloat16 [4096, 1024], P('shard'), may hold values from -0.09375 to 0.09375
- output_bias: bfloat16 [1024], P('shard'), may hold values from -3 to 3
Outputs:
- outputs: bfloat16 [8, 1024, 1024], P('replica', 'shard')
- in_grad: bfloat16 [8, 1024, 1024], P('replica', 'shard')
- grad_ln_gain_attn: float32 [1024], P('shard')
- grad_ln_bias_attn: float32 [1024], P('shard')
- grad_ln_gain_mlp: float32 [1024], P('shard')
- grad_ln_bias_mlp: float32 [1024], P('shard')
- grad_qkv_weight: float32 [1024, 3072], P('shard')
- grad_qkv_bias: float32 [3072], P('shard')
- grad_out_weight: float32 [1024, 1024], P('shard')
- grad_up_weight: float32 [1024, 4096], P('shard')
- grad_up_bias: float32 [4096], P('shard')
- grad_down_weight: float32 [4096, 1024], P('shard')
- grad_output_bias: float32 [1024], P('shard')
Inputs may be any that keep to these rules, and one draw needn't show every extreme that they name: `segment_ids`: in every sequence the document numbers never fall and run through 0 to 2; every document has 1 to 512 tokens, one exactly 512.
All inputs are finite; a program needn't handle non-finite values.
Results may differ from a plain program's by a relative error of at most 0.012.
Values may be sent and summed in bfloat16 or wider, within the bound.
A program may use at most 256 MiB of HBM per device.

v0:
```python
from functools import partial

import jax
import jax.numpy as jnp
from jax import lax
from jax.sharding import PartitionSpec as P

D = 1024
FF = 4096
HEADS = 16
HEAD = 64
ROT = 16
DOCS = 3


def layer_norm(values, gain, shift):
    centered = values - jnp.mean(values, axis=-1, keepdims=True)
    variance = jnp.mean(centered * centered, axis=-1, keepdims=True)
    return centered * lax.rsqrt(variance + 1e-05) * gain + shift


def exact_gelu(values):
    return jax.nn.gelu(values, approximate=False)


def doc_positions(segment_row):
    documents = jnp.arange(DOCS, dtype=jnp.int32)
    member = (segment_row[:, None] == documents[None, :]).astype(jnp.int32)
    counts = jnp.sum(member, axis=0)
    starts = jnp.cumsum(counts) - counts
    doc_start = jnp.sum(member * starts[None, :], axis=1)
    return jnp.arange(segment_row.shape[0], dtype=jnp.int32) - doc_start


def rotate(features, positions):
    half_rot = ROT // 2
    inv_freq = 1.0 / 10000.0 ** (jnp.arange(half_rot, dtype=jnp.float32) * 2.0 / ROT)
    angles = positions.astype(jnp.float32)[..., None] * inv_freq
    cosine = jnp.cos(angles)[..., None, :]
    sine_part = jnp.sin(angles)[..., None, :]
    front_half = features[..., :half_rot]
    back_half = features[..., half_rot:ROT]
    return jnp.concatenate(
        [
            front_half * cosine - back_half * sine_part,
            back_half * cosine + front_half * sine_part,
            features[..., ROT:],
        ],
        axis=-1,
    )


def masked_scores(queries, key_rows, segment_row, first_row):
    local_len = queries.shape[0]
    query_at = first_row + jnp.arange(local_len, dtype=jnp.int32)
    key_at = jnp.arange(key_rows.shape[0], dtype=jnp.int32)
    query_doc = lax.dynamic_slice_in_dim(segment_row, first_row, local_len, 0)
    allowed = (key_at[None, :] <= query_at[:, None]) & (segment_row[None, :] == query_doc[:, None])
    score_scale = queries.shape[-1] ** (-0.5)
    scores = (
        jnp.einsum("qhd,khd->hqk", queries, key_rows, preferred_element_type=jnp.float32)
        * score_scale
    )
    return jnp.where(allowed[None], scores, -1e30)


def attend_forward(first_row, element):
    queries, key_rows, value_rows, segment_row = element
    scores = masked_scores(queries, key_rows, segment_row, first_row)
    row_max = jnp.max(scores, axis=-1, keepdims=True)
    shifted_exp = jnp.exp(scores - row_max)
    row_sum = jnp.sum(shifted_exp, axis=-1, keepdims=True)
    probs = (shifted_exp / row_sum).astype(jnp.bfloat16)
    context = jnp.einsum("hqk,khd->qhd", probs, value_rows, preferred_element_type=jnp.float32)
    return (context.astype(jnp.bfloat16), row_max + jnp.log(row_sum))


def attend_backward(first_row, element):
    queries, key_rows, value_rows, segment_row, log_norm, grad_context = element
    scores = masked_scores(queries, key_rows, segment_row, first_row)
    weights = jnp.exp(scores - log_norm)
    grad_probs = jnp.einsum(
        "qhd,khd->hqk", grad_context, value_rows, preferred_element_type=jnp.float32
    )
    row_inner = jnp.sum(weights * grad_probs, axis=-1, keepdims=True)
    grad_scores = (weights * (grad_probs - row_inner)).astype(jnp.bfloat16)
    score_scale = queries.shape[-1] ** (-0.5)
    grad_query = (
        jnp.einsum("hqk,khd->qhd", grad_scores, key_rows, preferred_element_type=jnp.float32)
        * score_scale
    )
    grad_key = (
        jnp.einsum("hqk,qhd->khd", grad_scores, queries, preferred_element_type=jnp.float32)
        * score_scale
    )
    grad_value = jnp.einsum(
        "hqk,qhd->khd",
        weights.astype(jnp.bfloat16),
        grad_context,
        preferred_element_type=jnp.float32,
    )
    return (grad_query, grad_key, grad_value)


def shards(
    inputs,
    out_grad,
    segment_ids,
    ln_gain_attn,
    ln_bias_attn,
    ln_gain_mlp,
    ln_bias_mlp,
    qkv_weight,
    qkv_bias,
    out_weight,
    up_weight,
    up_bias,
    down_weight,
    output_bias,
):
    seq_count, local_len, model_width = inputs.shape
    token_count = seq_count * local_len
    first_row = lax.axis_index("shard") * local_len
    group_ratio = FF // D
    flat_in = inputs.reshape(token_count, model_width).astype(jnp.float32)
    gain_attn, shift_attn, gain_mlp, shift_mlp, qkv_shift, up_shift, out_shift = (
        lax.all_gather(ln_gain_attn, "shard", axis=0, tiled=True),
        lax.all_gather(ln_bias_attn, "shard", axis=0, tiled=True),
        lax.all_gather(ln_gain_mlp, "shard", axis=0, tiled=True),
        lax.all_gather(ln_bias_mlp, "shard", axis=0, tiled=True),
        lax.all_gather(qkv_bias, "shard", axis=0, tiled=True),
        lax.all_gather(up_bias, "shard", axis=0, tiled=True),
        lax.all_gather(output_bias, "shard", axis=0, tiled=True),
    )
    attn_float, attn_pullback = jax.vjp(
        layer_norm, flat_in, gain_attn.astype(jnp.float32), shift_attn.astype(jnp.float32)
    )
    mlp_float, mlp_pullback = jax.vjp(
        layer_norm, flat_in, gain_mlp.astype(jnp.float32), shift_mlp.astype(jnp.float32)
    )
    attn_normed = attn_float.astype(jnp.bfloat16)
    mlp_normed = mlp_float.astype(jnp.bfloat16)
    pieces = (
        lax.all_gather(qkv_weight, "shard", axis=0, tiled=True),
        lax.all_gather(up_weight, "shard", axis=0, tiled=True),
    )
    qkv_sum = jnp.dot(attn_normed, pieces[0], preferred_element_type=jnp.float32)
    up_sum = jnp.dot(mlp_normed, pieces[1], preferred_element_type=jnp.float32)
    qkv_parts = (qkv_sum + qkv_shift.astype(jnp.float32)).reshape(
        seq_count, local_len, 3, HEADS, HEAD
    )
    all_positions = jax.vmap(doc_positions)(segment_ids)
    own_positions = lax.dynamic_slice_in_dim(all_positions, first_row, local_len, 1)

    def rotate_pair(query_part, key_part):
        return (rotate(query_part, own_positions), rotate(key_part, own_positions))

    (query_rot, key_rot), rotate_pullback = jax.vjp(
        rotate_pair, qkv_parts[:, :, 0], qkv_parts[:, :, 1]
    )
    query_low = query_rot.astype(jnp.bfloat16)
    key_low = key_rot.astype(jnp.bfloat16)
    value_low = qkv_parts[:, :, 2].astype(jnp.bfloat16)
    key_all, value_all = (
        lax.all_gather(key_low, "shard", axis=1, tiled=True),
        lax.all_gather(value_low, "shard", axis=1, tiled=True),
    )
    context_seq, log_norms = lax.map(
        partial(attend_forward, first_row), (query_low, key_all, value_all, segment_ids)
    )
    context_low = context_seq.reshape(token_count, model_width)
    hidden_act, gelu_pullback = jax.vjp(exact_gelu, up_sum + up_shift.astype(jnp.float32))
    hidden_low = hidden_act.astype(jnp.bfloat16)
    down_grouped = down_weight.reshape(-1, group_ratio * model_width)
    pieces = (
        lax.all_gather(out_weight, "shard", axis=0, tiled=True),
        lax.all_gather(down_grouped, "shard", axis=0, tiled=True),
    )
    piece_rows = pieces[0].shape[0]
    down_rows = pieces[1].reshape(piece_rows * group_ratio, model_width)
    mixed = jnp.dot(context_low, pieces[0], preferred_element_type=jnp.float32) + jnp.dot(
        hidden_low, down_rows, preferred_element_type=jnp.float32
    )
    result = flat_in + mixed + out_shift.astype(jnp.float32)
    outputs = result.astype(jnp.bfloat16).reshape(seq_count, local_len, model_width)
    grad_low = out_grad.reshape(token_count, model_width)
    grad_float = grad_low.astype(jnp.float32)
    grad_out_shift = jnp.sum(grad_float, axis=0)
    grad_out_weight = jnp.einsum(
        "tk,tn->kn", context_low, grad_low, preferred_element_type=jnp.float32
    )
    grad_down_weight = jnp.einsum(
        "tk,tn->kn", hidden_low, grad_low, preferred_element_type=jnp.float32
    )
    out_shares = (
        lax.psum_scatter(grad_out_weight, "shard", scatter_dimension=0, tiled=True),
        lax.psum_scatter(grad_down_weight, "shard", scatter_dimension=0, tiled=True),
        lax.psum_scatter(grad_out_shift, "shard", scatter_dimension=0, tiled=True),
    )
    out_totals = lax.psum((out_shares[0], out_shares[1], out_shares[2]), "replica")
    pieces = (
        lax.all_gather(out_weight, "shard", axis=0, tiled=True),
        lax.all_gather(down_grouped, "shard", axis=0, tiled=True),
    )
    piece_rows = pieces[0].shape[0]
    down_rows = pieces[1].reshape(piece_rows * group_ratio, model_width)
    context_part = jnp.einsum("tn,kn->tk", grad_low, pieces[0], preferred_element_type=jnp.float32)
    hidden_part = jnp.einsum("tn,kn->tk", grad_low, down_rows, preferred_element_type=jnp.float32)
    context_grad_low = context_part.astype(jnp.bfloat16).reshape(seq_count, local_len, HEADS, HEAD)
    hidden_grad_low = gelu_pullback(hidden_part)[0].astype(jnp.bfloat16)
    key_back, value_back = (key_all, value_all)
    grad_query, key_part, value_part = lax.map(
        partial(attend_backward, first_row),
        (query_low, key_back, value_back, segment_ids, log_norms, context_grad_low),
    )
    grad_key, grad_value = (
        lax.psum_scatter(key_part, "shard", scatter_dimension=1, tiled=True),
        lax.psum_scatter(value_part, "shard", scatter_dimension=1, tiled=True),
    )
    query_pre, key_pre = rotate_pullback((grad_query, grad_key))
    grad_qkv = (
        jnp.stack([query_pre, key_pre, grad_value], axis=2)
        .reshape(token_count, 3 * model_width)
        .astype(jnp.bfloat16)
    )
    grad_qkv_shift = jnp.sum(grad_qkv.astype(jnp.float32), axis=0)
    grad_up_shift = jnp.sum(hidden_grad_low.astype(jnp.float32), axis=0)
    grad_qkv_weight = jnp.einsum(
        "tk,tn->kn", attn_normed, grad_qkv, preferred_element_type=jnp.float32
    )
    grad_up_weight = jnp.einsum(
        "tk,tn->kn", mlp_normed, hidden_grad_low, preferred_element_type=jnp.float32
    )
    pieces = (
        lax.all_gather(qkv_weight, "shard", axis=0, tiled=True),
        lax.all_gather(up_weight, "shard", axis=0, tiled=True),
    )
    attn_part = jnp.einsum("tn,kn->tk", grad_qkv, pieces[0], preferred_element_type=jnp.float32)
    mlp_part = jnp.einsum(
        "tn,kn->tk", hidden_grad_low, pieces[1], preferred_element_type=jnp.float32
    )
    attn_input, grad_gain_attn, grad_shift_attn = attn_pullback(attn_part)
    mlp_input, grad_gain_mlp, grad_shift_mlp = mlp_pullback(mlp_part)
    in_grad = (
        (grad_float + attn_input + mlp_input)
        .astype(jnp.bfloat16)
        .reshape(seq_count, local_len, model_width)
    )
    in_shares = (
        lax.psum_scatter(grad_gain_attn, "shard", scatter_dimension=0, tiled=True),
        lax.psum_scatter(grad_shift_attn, "shard", scatter_dimension=0, tiled=True),
        lax.psum_scatter(grad_gain_mlp, "shard", scatter_dimension=0, tiled=True),
        lax.psum_scatter(grad_shift_mlp, "shard", scatter_dimension=0, tiled=True),
        lax.psum_scatter(grad_qkv_weight, "shard", scatter_dimension=0, tiled=True),
        lax.psum_scatter(grad_qkv_shift, "shard", scatter_dimension=0, tiled=True),
        lax.psum_scatter(grad_up_weight, "shard", scatter_dimension=0, tiled=True),
        lax.psum_scatter(grad_up_shift, "shard", scatter_dimension=0, tiled=True),
    )
    in_totals = lax.psum(
        (
            in_shares[0],
            in_shares[1],
            in_shares[2],
            in_shares[3],
            in_shares[4],
            in_shares[5],
            in_shares[6],
            in_shares[7],
        ),
        "replica",
    )
    return (
        outputs,
        in_grad,
        in_totals[0],
        in_totals[1],
        in_totals[2],
        in_totals[3],
        in_totals[4],
        in_totals[5],
        out_totals[0],
        in_totals[6],
        in_totals[7],
        out_totals[1],
        out_totals[2],
    )


def solution(mesh):
    placed = (
        P("replica", "shard", None),
        P("replica", "shard", None),
        P("replica", None),
        P("shard"),
        P("shard"),
        P("shard"),
        P("shard"),
        P("shard", None),
        P("shard"),
        P("shard", None),
        P("shard", None),
        P("shard"),
        P("shard", None),
        P("shard"),
    )
    return jax.shard_map(
        shards,
        mesh=mesh,
        in_specs=placed,
        out_specs=(
            P("replica", "shard", None),
            P("replica", "shard", None),
            P("shard"),
            P("shard"),
            P("shard"),
            P("shard"),
            P("shard", None),
            P("shard"),
            P("shard", None),
            P("shard", None),
            P("shard"),
            P("shard", None),
            P("shard"),
        ),
        check_vma=False,
    )
```

profile of v0, /device:TPU:0, one launch (start us, length us, event | category | flops | bytes accessed | tf_op | source)
XLA Modules:
  0.0 1781.4 jit_solution(8662586912904173164)
XLA Ops:
  9.4 14.7 all-gather.3
  24.8 11.0 all-gather.2
  36.4 8.2 all-gather.1
  50.4 77.4 %all-gather.14.cloned.1.call-done = bf16[1024,3072]{1,0:T(8,128)(2,1)} async-done(((bf16[256,3072]{1,0:T(8,128)(2,1)}), bf16[1024,3072]{1,0:T(8,128)(2,1)}) %all-gather.14.cloned.1.call-update) | async-done | bytes 6291472 | tf_op jit(solution)/shard_map/all_gather | solution.py:144
  146.2 27.3 %all-gather.18.cloned.1.call-done = bf16[1024,1024]{1,0:T(8,128)(2,1)} async-done(((bf16[256,1024]{1,0:T(8,128)(2,1)}), bf16[1024,1024]{1,0:T(8,128)(2,1)}) %all-gather.18.cloned.1.call-update) | async-done | bytes 2097168 | tf_op jit(solution)/shard_map/all_gather | solution.py:176
  177.3 43.3 %all-gather.16.cloned.1.call-done = bf16[1,1024,16,64]{1,3,2,0:T(8,128)(2,1)} async-done(((bf16[1,256,16,64]{1,3,2,0:T(8,128)(2,1)}), bf16[1,1024,16,64]{1,3,2,0:T(8,128)(2,1)}) %all-gather.16.cloned.1.call-update) | async-done | bytes 2097168 | tf_op jit(solution)/shard_map/all_gather | solution.py:165
  231.9 35.2 %all-gather.24.cloned.1.call-done = bf16[1,1024,1,16,64]{1,4,3,2,0:T(8,128)(2,1)} async-done(((bf16[1,256,1,16,64]{1,4,3,2,0:T(8,128)(2,1)}), bf16[1,1024,1,16,64]{1,4,3,2,0:T(8,128)(2,1)}) %all-gather.24.cloned.1.call-update) | async-done | bytes 2097168 | tf_op jit(solution)/shard_map/all_gather | solution.py:166
  267.2 15.4 multiply_reduce_fusion
  284.8 7.8 multiply_convert_fusion
  300.1 9.4 fusion.12
  311.2 7.5 fusion.41
  322.9 14.4 all_gather.53
  337.3 8.8 all-gather.5
  346.1 11.4 all-gather.4
  357.5 59.8 %all-gather.22.cloned.1.call-done = bf16[1024,4096]{1,0:T(8,128)(2,1)} async-done(((bf16[256,4096]{1,0:T(8,128)(2,1)}), bf16[1024,4096]{1,0:T(8,128)(2,1)}) %all-gather.22.cloned.1.call-update) | async-done | bytes 8388624 | tf_op jit(solution)/shard_map/all_gather | solution.py:177
  417.3 14.3 reshape.567
  431.5 135.1 %all-gather.20.cloned.1.call-done = bf16[1024,4096]{1,0:T(8,128)(2,1)} async-done(((bf16[256,4096]{1,0:T(8,128)(2,1)}), bf16[1024,4096]{1,0:T(8,128)(2,1)}) %all-gather.20.cloned.1.call-update) | async-done | bytes 8388624 | tf_op jit(solution)/shard_map/all_gather | solution.py:145
  566.6 15.8 multiply_convert_fusion.1
  582.4 7.7 convert_reduce_fusion
  591.4 8.3 fusion.92
  600.2 8.1 fusion.66
  616.9 27.0 %reduce-scatter.7.cloned.1.call-done = f32[1,256,16,64]{1,3,2,0:T(8,128)} async-done(((f32[1,1024,16,64]{1,3,2,0:T(8,128)}), f32[1,256,16,64]{1,3,2,0:T(8,128)}) %reduce-scatter.7.cloned.1.call-update) | async-done | bytes 1048592 | tf_op jit(solution)/shard_map/reduce_scatter | solution.py:217
  647.2 76.4 %reduce-scatter.9.cloned.1.call-done = f32[1,256,16,64]{1,3,2,0:T(8,128)} async-done(((f32[1,1024,16,64]{1,3,2,0:T(8,128)}), f32[1,256,16,64]{1,3,2,0:T(8,128)}) %reduce-scatter.9.cloned.1.call-update) | async-done | bytes 1048592 | tf_op jit(solution)/shard_map/reduce_scatter | solution.py:218
  725.4 7.7 fusion.62
  733.2 70.0 %reduce-scatter.13.cloned.1.call-done = f32[256,1024]{1,0:T(8,128)} async-done(((f32[1024,1024]{1,0:T(8,128)}), f32[256,1024]{1,0:T(8,128)}) %reduce-scatter.13.cloned.1.call-update) | async-done | bytes 1048592 | tf_op jit(solution)/shard_map/reduce_scatter | solution.py:196
  803.2 283.2 %reduce-scatter.15.cloned.1.call-done = f32[256,4096]{1,0:T(8,128)} async-done(((f32[1024,4096]{1,0:T(8,128)}), f32[256,4096]{1,0:T(8,128)}) %reduce-scatter.15.cloned.1.call-update) | async-done | bytes 4194320 | tf_op jit(solution)/shard_map/reduce_scatter | solution.py:256
  1086.4 283.4 %reduce-scatter.17.cloned.1.call-done = f32[1024,1024]{1,0:T(8,128)} async-done(((f32[4096,1024]{1,0:T(8,128)}), f32[1024,1024]{1,0:T(8,128)}) %reduce-scatter.17.cloned.1.call-update) | async-done | bytes 4194320 | tf_op jit(solution)/shard_map/reduce_scatter | solution.py:197
  1369.8 215.0 %reduce-scatter.11.cloned.1.call-done = f32[256,3072]{1,0:T(8,128)} async-done(((f32[1024,3072]{1,0:T(8,128)}), f32[256,3072]{1,0:T(8,128)}) %reduce-scatter.11.cloned.1.call-update) | async-done | bytes 3145744 | tf_op jit(solution)/shard_map/reduce_scatter | solution.py:254
  1585.4 10.8 all-gather.6
  1622.0 16.8 all-reduce.15
  1639.3 23.6 %all-reduce.13 = (f32[256]{0:T(256)}, f32[256]{0:T(256)}, f32[256]{0:T(256)}, f32[256]{0:T(256)}, f32[768]{0:T(1024)}, /*index=5*/f32[1024]{0:T(1024)}, f32[256]{0:T(256)}) all-reduce(f32[256]{0:T(256)S(1)} %dynamic-slice.3, f32[256]{0:T(256)S(1)} %dynamic-slice.5, ...), channel_id=1, replica_groups=mesh['replica'=8,'shard'=4] {'replica'}, use_global_device_ids=true, to_apply=%region_16.17 | all-reduce | flops 3072 | bytes 24576 | tf_op jit(solution)/shard_map/psum | solution.py:259
  1662.9 101.0 %all-reduce.18.cloned.1.call-done = (f32[256,3072]{1,0:T(8,128)}, f32[256,1024]{1,0:T(8,128)}, f32[256,4096]{1,0:T(8,128)}, f32[1024,1024]{1,0:T(8,128)}) async-done(((f32[256,3072]{1,0:T(8,128)}, f32[256,1024]{1,0:T(8,128)}, f32[256,4096]{1,0:T(8,128)}, f32[1024,1024]{1,0:T(8,128)}), (f32[256,3072]{1,0:T(8,128)}, f32[256,1024]{1,0:T(8,128)}, f32[256,4096]{1,0:T(8,128)}, ...) | async-done | bytes 12582928 | tf_op jit(solution)/shard_map/psum | solution.py:259
  (198 shorter events, 109.1 us)
Async XLA Ops:
  7.2 120.6 %all-gather.14.cloned.1.call-start = ((), (), s32[]{:S(2)}) async-start(), calls=%async_computation.6 | async-start | bytes 7864320 | tf_op jit(solution)/shard_map/all_gather | solution.py:144
  7.9 165.6 %all-gather.18.cloned.1.call-start = ((), (), s32[]{:S(2)}) async-start(), calls=%async_computation.8 | async-start | bytes 2621440 | tf_op jit(solution)/shard_map/all_gather | solution.py:176
  8.7 212.0 %all-gather.16.cloned.1.call-start = ((), (), s32[]{:S(2)}) async-start(), calls=%async_computation.7 | async-start | bytes 2621440 | tf_op jit(solution)/shard_map/all_gather | solution.py:165
  50.3 84.1 %copy-start.37 = (f32[256]{0:T(256)}, f32[256]{0:T(256)S(1)}, u32[]{:S(2)}) copy-start(f32[256]{0:T(256)S(1)} %fusion.53) | copy-start | bytes 3076
  50.3 84.1 %copy-start.32 = (f32[256]{0:T(256)}, f32[256]{0:T(256)S(1)}, u32[]{:S(2)}) copy-start(f32[256]{0:T(256)S(1)} %fusion.89) | copy-start | bytes 3076
  50.4 86.7 %copy-start.28 = (f32[256,8]{0,1:T(8,128)}, f32[256,8]{0,1:T(8,128)S(1)}, u32[]{:S(2)}) copy-start(f32[256,8]{0,1:T(8,128)S(1)} %get-tuple-element.122) | copy-start | bytes 24580
  50.4 86.7 %copy-start.29 = (f32[256,8]{0,1:T(8,128)}, f32[256,8]{0,1:T(8,128)S(1)}, u32[]{:S(2)}) copy-start(f32[256,8]{0,1:T(8,128)S(1)} %get-tuple-element.123) | copy-start | bytes 24580
  139.6 127.6 %all-gather.24.cloned.1.call-start = ((), (), s32[]{:S(2)}) async-start(), calls=%async_computation.17 | async-start | bytes 2621440 | tf_op jit(solution)/shard_map/all_gather | solution.py:166
  140.5 33.0 %copy-start.5 = (bf16[1,256,1024]{2,1,0:T(8,128)(2,1)S(1)}, bf16[1,256,1024]{2,1,0:T(8,128)(2,1)}, u32[]{:S(2)}) copy-start(bf16[1,256,1024]{2,1,0:T(8,128)(2,1)} %param.15) | copy-start | bytes 1572868
  140.5 276.7 %all-gather.22.cloned.1.call-start = ((), (), s32[]{:S(2)}) async-start(), calls=%async_computation.10 | async-start | bytes 10485760 | tf_op jit(solution)/shard_map/all_gather | solution.py:177
  145.0 75.6 %copy-start.21 = (bf16[256,16,8]{0,2,1:T(8,128)(2,1)S(1)}, bf16[256,16,8]{0,2,1:T(8,128)(2,1)}, u32[]{:S(2)}) copy-start(bf16[256,16,8]{0,2,1:T(8,128)(2,1)} %get-tuple-element.110) | copy-start | bytes 196612
  145.0 75.6 %copy-start.23 = (bf16[256,16,8]{0,2,1:T(8,128)(2,1)S(1)}, bf16[256,16,8]{0,2,1:T(8,128)(2,1)}, u32[]{:S(2)}) copy-start(bf16[256,16,8]{0,2,1:T(8,128)(2,1)} %get-tuple-element.111) | copy-start | bytes 196612
  145.0 421.5 %all-gather.20.cloned.1.call-start = ((), (), s32[]{:S(2)}) async-start(), calls=%async_computation.9 | async-start | bytes 10485760 | tf_op jit(solution)/shard_map/all_gather | solution.py:145
  145.6 498.3 %reduce-scatter.7.cloned.1.call-start = ((), (), s32[]{:S(2)}) async-start(), calls=%async_computation.11 | async-start | bytes 5242880 | tf_op jit(solution)/shard_map/reduce_scatter | solution.py:217
  177.3 47.9 %copy-start.12 = (bf16[256,16,48]{0,2,1:T(8,128)(2,1)}, bf16[256,16,48]{0,2,1:T(8,128)(2,1)S(1)}, u32[]{:S(2)}) copy-start(bf16[256,16,48]{0,2,1:T(8,128)(2,1)S(1)} %fusion.83) | copy-start | bytes 1179652
  267.2 15.4 slice-start
  267.2 15.4 slice-start.1
  267.2 16.4 slice-start.2
  267.2 17.6 slice-start.3
  299.4 424.1 %reduce-scatter.9.cloned.1.call-start = ((), (), s32[]{:S(2)}) async-start(), calls=%async_computation.12 | async-start | bytes 5242880 | tf_op jit(solution)/shard_map/reduce_scatter | solution.py:218
  309.6 493.6 %reduce-scatter.13.cloned.1.call-start = ((), (), s32[]{:S(2)}) async-start(), calls=%async_computation.14 | async-start | bytes 5242880 | tf_op jit(solution)/shard_map/reduce_scatter | solution.py:196
  322.2 15.1 copy-start.41
  322.2 23.9 %copy-start.42 = (bf16[256]{0:T(256)(128)(2,1)S(1)}, bf16[256]{0:T(256)(128)(2,1)}, u32[]{:S(2)}) copy-start(bf16[256]{0:T(256)(128)(2,1)} %param.19) | copy-start | bytes 1540
  322.3 764.1 %reduce-scatter.15.cloned.1.call-start = ((), (), s32[]{:S(2)}) async-start(), calls=%async_computation.15 | async-start | bytes 20971520 | tf_op jit(solution)/shard_map/reduce_scatter | solution.py:256
  357.5 209.1 %copy-start.2 = (bf16[1,256,1024]{2,1,0:T(8,128)(2,1)S(1)}, bf16[1,256,1024]{2,1,0:T(8,128)(2,1)}, u32[]{:S(2)}) copy-start(bf16[1,256,1024]{2,1,0:T(8,128)(2,1)} %param.14) | copy-start | bytes 1572868
  357.5 209.1 %copy-start.33 = (f32[256]{0:T(256)S(1)}, f32[256]{0:T(256)}, u32[]{:S(2)}) copy-start(f32[256]{0:T(256)} %copy-done.32) | copy-start | bytes 3076
  566.6 15.9 copy-start.3
  582.4 17.7 copy-start.15
  599.7 770.1 %reduce-scatter.17.cloned.1.call-start = ((), (), s32[]{:S(2)}) async-start(), calls=%async_computation.16 | async-start | bytes 20971520 | tf_op jit(solution)/shard_map/reduce_scatter | solution.py:197
  608.3 976.4 %reduce-scatter.11.cloned.1.call-start = ((), (), s32[]{:S(2)}) async-start(), calls=%async_computation.13 | async-start | bytes 15728640 | tf_op jit(solution)/shard_map/reduce_scatter | solution.py:254
  616.9 29.5 %slice-start.4 = ((f32[1,256,16,64]{1,3,2,0:T(8,128)}), f32[1,256,16,48]{1,3,2,0:T(8,128)S(1)}, s32[]{:S(2)}) async-start(f32[1,256,16,64]{1,3,2,0:T(8,128)} %copy-done.9), calls=%async_computation.23 | async-start | bytes 1572864 | tf_op jit(solution)/shard_map/transpose(jvp())/split | solution.py:43
  733.1 1030.8 %all-reduce.18.cloned.1.call-start = ((), (), s32[]{:S(2)}) async-start(), calls=%async_computation.18 | async-start | bytes 25165824 | tf_op jit(solution)/shard_map/psum | solution.py:259
  (31 other events, 130.3 us)
Sparse Core Ops, SparseCore 0:
  9.6 118.1 all-gather.13
  129.4 44.1 all-gather.17
  175.7 44.9 all-gather.15
  222.6 44.4 all-gather.23
  269.1 148.0 all-gather.21
  418.7 147.8 all-gather.19
  568.9 74.9 reduce-scatter.6
  646.3 77.2 reduce-scatter.8
  725.9 77.2 reduce-scatter.12
  805.5 280.7 reduce-scatter.14
  1088.7 281.0 reduce-scatter.16
  1372.1 212.5 reduce-scatter.10
  1589.3 174.6 all-reduce.17
where the time goes:
time: 1790 us; the launch traced here: 1780 us
  waiting for transfers between devices  1440 us (80%)
  matrix products  126 us (7%)
  blocking collectives  120 us (7%)
  local copies, waits for them, and re-layouts  55.4 us (3%)
  other arithmetic  26.3 us (1%)
    reduce_scatter x1, waiting for transfers between devices, shards(): lax.psum_scatter(grad_down_weight, 'shard', scatter_dimension=0, tiled=True)  283 us
    reduce_scatter x1, waiting for transfers between devices, shards(): lax.psum_scatter(grad_up_weight, 'shard', scatter_dimension=0, tiled=True)  283 us
    reduce_scatter x1, waiting for transfers between devices, shards(): lax.psum_scatter(grad_qkv_weight, 'shard', scatter_dimension=0, tiled=True)  215 us
    all_gather x1, waiting for transfers between devices, shards(): lax.all_gather(up_weight, 'shard', axis=0, tiled=True)  135 us
    psum x1, waiting for transfers between devices, shards(): lax.psum((in_shares[0], in_shares[1], in_shares[2], in_shares[3], in_shar...  101 us
    all_gather x1, waiting for transfers between devices, shards(): lax.all_gather(qkv_weight, 'shard', axis=0, tiled=True)  77.4 us
    reduce_scatter x1, waiting for transfers between devices, shards(): lax.psum_scatter(value_part, 'shard', scatter_dimension=1, tiled=True)  76.4 us
    reduce_scatter x1, waiting for transfers between devices, shards(): lax.psum_scatter(grad_out_weight, 'shard', scatter_dimension=0, tiled=True)  70 us
  transfers between devices with their start and end apart: 13, of which 13 were waited for; matrix products, arithmetic and copies ran while one was open for 10% of the time, Pallas kernels for 0%

commit v1 on v0

v1 whole, which is shorter than its diff:
```python
import math
from functools import partial

import jax
import jax.numpy as jnp
from jax import lax
from jax.experimental import pallas as pl
from jax.experimental.pallas import tpu as pltpu
from jax.sharding import PartitionSpec as P

D = 1024
FF = 4096
HEADS = 16
HEAD = 64
ROT = 16
Z = 4
LOC = 256
TOK = 1024
PAIRS = 2
QB = 128
KB = 640
EPS = 1e-05
BF = jnp.bfloat16
F32 = jnp.float32
MESH = pl.DeviceIdType.MESH
NSEM = 256
STAGE = 4


def bit_of(value, place):
    return lax.rem(lax.div(value, 1 << place), 2)


def flip(value, place):
    return value + (1 - 2 * bit_of(value, place)) * (1 << place)


def nn(a, b):
    return jnp.dot(a, b, preferred_element_type=F32)


def nt(a, b):
    return lax.dot_general(a, b, (((1,), (1,)), ((), ())), preferred_element_type=F32)


def tn(a, b):
    return lax.dot_general(a, b, (((0,), (0,)), ((), ())), preferred_element_type=F32)


def blk(i, n):
    return pl.ds(pl.multiple_of(i * n, n), n)


class Count:
    def __init__(self):
        self.used = 0

    def take(self, n):
        first = self.used
        self.used += n
        assert self.used <= NSEM
        return first


def layer(
    replicas,
    stage,
    x_in,
    og_in,
    qkv_w,
    up_w,
    out_w,
    down_w,
    vec_in,
    upb,
    start,
    tab_c,
    tab_a,
    tab_b,
    outputs,
    in_grad,
    f_qkv,
    f_up,
    f_out,
    f_down,
    vec_out,
    x_all,
    og_all,
    vec_all,
    wqkv,
    wup,
    wout,
    wdown,
    attn_n,
    mlp_n,
    mean_s,
    rstd_s,
    q_s,
    k_s,
    v_s,
    ctx,
    lse,
    h32,
    g32,
    acc,
    hidden,
    dgelu,
    part,
    own,
    zrecv,
    zrelay,
    gctx,
    dq,
    dk,
    dv,
    dqkv,
    g_qkv,
    g_up,
    g_out,
    g_down,
    t_qkv,
    t_up,
    t_out,
    t_down,
    vsum,
    vrecv,
    ssem,
    rsem,
    lsem,
):
    r = lax.axis_index("replica")
    z = lax.axis_index("shard")
    bits = int(math.log2(replicas))
    nb = min(bits, 4)
    chunks = 1 << nb
    sends, recvs, locals_ = Count(), Count(), Count()
    pending = []

    def remote(src, dst, s, v, dev):
        return pltpu.make_async_remote_copy(
            src_ref=src,
            dst_ref=dst,
            send_sem=ssem.at[s],
            recv_sem=rsem.at[v],
            device_id=dev,
            device_id_type=MESH,
        )

    def go(src, dst, s, v, dev, when=None):
        copy = remote(src, dst, s, v, dev)
        if when is None:
            copy.start()
        else:
            pl.when(when)(copy.start)
        pending.append((copy, when))

    def arrived(dst, v, when=None):
        copy = remote(dst, dst, 0, v, (r, z))
        if when is None:
            copy.wait_recv()
        else:
            pl.when(when)(copy.wait_recv)

    def local(src, dst):
        copy = pltpu.make_async_copy(src, dst, lsem.at[locals_.take(1)])
        copy.start()
        return copy

    barrier = pltpu.get_barrier_semaphore()
    for step in range(1, Z):
        pl.semaphore_signal(
            barrier, inc=1, device_id=(r, lax.rem(z + step, Z)), device_id_type=MESH
        )
    for b in range(bits):
        pl.semaphore_signal(barrier, inc=1, device_id=(flip(r, b), z), device_id_type=MESH)
    pl.semaphore_wait(barrier, Z - 1 + bits)

    order_a = list(range(nb))
    order_b = [0, *reversed(range(1, nb))]

    def index_of(order):
        return sum(bit_of(r, b) * (1 << (nb - 1 - k)) for k, b in enumerate(order))

    idx_a, idx_b = index_of(order_a), index_of(order_b)
    cr = LOC // chunks

    up_v, qkv_v, vec_v = recvs.take(Z), recvs.take(3 * Z), recvs.take(Z)
    vec_own = local(vec_in, vec_all.at[blk(z, 16)])
    for step in (1, 3, 2):
        t = lax.rem(z + step, Z)
        go(vec_in, vec_all.at[blk(z, 16)], sends.take(1), vec_v + z, (r, t))
        go(
            up_w.at[blk(idx_a, cr), blk(t, 1024)],
            wup.at[pl.ds(pl.multiple_of(z * LOC + idx_a * cr, cr), cr)],
            sends.take(1),
            up_v + z,
            (r, t),
        )
        for s in range(3):
            go(
                qkv_w.at[blk(idx_b, cr), pl.ds(pl.multiple_of(s * D + t * 256, 256), 256)],
                wqkv.at[pl.ds(pl.multiple_of(z * LOC + idx_b * cr, cr), cr), pl.ds(s * 256, 256)],
                sends.take(1),
                qkv_v + z * 3 + s,
                (r, t),
            )
    own_up = local(up_w.at[:, blk(z, 1024)], wup.at[blk(z, LOC)])
    own_qkv = [
        local(
            qkv_w.at[:, pl.ds(pl.multiple_of(s * D + z * 256, 256), 256)],
            wqkv.at[blk(z, LOC), pl.ds(s * 256, 256)],
        )
        for s in range(3)
    ]

    SUB = 2

    class Gather:
        def __init__(self, src, buf):
            self.src, self.buf = src, buf
            self.v = recvs.take(Z * SUB)

        def rows(self, c, k):
            n = LOC // SUB
            return self.buf.at[pl.ds(pl.multiple_of(c * LOC + k * n, n), n)]

        def send(self):
            n = LOC // SUB
            for k in range(SUB):
                for d in (2, -2, 1, -1):
                    t = z + d
                    go(
                        self.src.at[pl.ds(k * n, n)],
                        self.rows(z, k),
                        sends.take(1),
                        self.v + z * SUB + k,
                        (r, jnp.clip(t, 0, Z - 1)),
                        (t >= 0) & (t < Z),
                    )

        def relay(self):
            for k in range(SUB):
                s = sends.take(1)
                for at, frm, to in ((2, 0, 3), (1, 3, 0)):
                    arrived(self.rows(frm, k), self.v + frm * SUB + k, z == at)
                    go(
                        self.rows(frm, k),
                        self.rows(frm, k),
                        s,
                        self.v + frm * SUB + k,
                        (r, to),
                        z == at,
                    )

        def wait(self, c):
            passed = ((z == 2) & (c == 0)) | ((z == 1) & (c == 3))
            for k in range(SUB):
                arrived(self.rows(c, k), self.v + c * SUB + k, jnp.logical_not(passed))

    near = [z, z + 1 - 2 * lax.rem(z, 2), z + 2 - 4 * lax.div(z, 2), 3 - z]
    gx, gg = Gather(x_in, x_all), Gather(og_in, og_all)
    gx.send()
    x_own = local(x_in, x_all.at[blk(z, LOC)])
    og_own = local(og_in, og_all.at[blk(z, LOC)])
    w_own = [local(out_w, wout), local(down_w, wdown)]

    ag_v = recvs.take(3 * 2 * nb)

    def weight_region(kind, zz, first, n):
        ref = wup if kind == 0 else wqkv
        return ref.at[pl.ds(pl.multiple_of(zz * LOC + first * cr, cr), n * cr)]

    def weight_step(k):
        for j in range(1, Z):
            zz = lax.rem(z + j, Z)
            for kind, order, idx in ((0, order_a, idx_a), (1, order_b, idx_b)):
                b = order[nb - 1 - k]
                size = 1 << k
                first = lax.div(idx, size) * size
                go(
                    weight_region(kind, zz, first, size),
                    weight_region(kind, zz, first, size),
                    sends.take(1),
                    ag_v + ((j - 1) * 2 + kind) * nb + k,
                    (flip(r, b), z),
                )

    def weight_wait(k):
        for j in range(1, Z):
            zz = lax.rem(z + j, Z)
            for kind, idx in ((0, idx_a), (1, idx_b)):
                size = 1 << k
                first = flip(lax.div(idx, size), 0) * size
                arrived(weight_region(kind, zz, first, size), ag_v + ((j - 1) * 2 + kind) * nb + k)

    for j in range(1, Z):
        zz = lax.rem(z + j, Z)
        arrived(vec_all.at[blk(zz, 16)], vec_v + zz)
        arrived(weight_region(0, zz, idx_a, 1), up_v + zz)
        for s in range(3):
            arrived(
                wqkv.at[pl.ds(pl.multiple_of(zz * LOC + idx_b * cr, cr), cr), pl.ds(s * 256, 256)],
                qkv_v + zz * 3 + s,
            )
    for k in range(nb):
        weight_step(k)
        if k == nb - 1:
            gx.relay()
        weight_wait(k)
    vec_own.wait()
    x_own.wait()
    og_own.wait()
    own_up.wait()
    for copy in own_qkv + w_own:
        copy.wait()
    for c in near[1:]:
        gx.wait(c)
    gg.send()

    if stage >= 2:
        def vector(row):
            return jnp.concatenate(
                [vec_all[16 * c : 16 * c + 16, :][row : row + 1, :] for c in range(Z)], axis=1
            ).astype(F32)

        def vector256(i):
            block = vec_all[pl.ds(pl.multiple_of(lax.div(i, 3) * 16, 16), 16), :].astype(F32)
            rows = lax.broadcasted_iota(jnp.int32, (16, 256), 0)
            return jnp.sum(jnp.where(rows == 4 + lax.rem(i, 3), block, 0.0), axis=0, keepdims=True)

        gain_a, bias_a, gain_m, bias_m, bias_o = [vector(i) for i in (0, 1, 2, 3, 7)]
        qkv_b = [vector256(s * Z + z) for s in range(3)]

        def norm(i, carry):
            rows = blk(i, 16)
            v = x_all[rows, :].astype(F32)
            mean = jnp.mean(v, axis=1, keepdims=True)
            cen = v - mean
            rstd = lax.rsqrt(jnp.mean(cen * cen, axis=1, keepdims=True) + EPS)
            xhat = cen * rstd
            attn_n[rows, :] = (xhat * gain_a + bias_a).astype(BF)
            mlp_n[rows, :] = (xhat * gain_m + bias_m).astype(BF)
            mean_s[rows, :] = mean
            rstd_s[rows, :] = rstd
            return carry

        lax.fori_loop(0, TOK // 16, norm, 0, unroll=2)

        def rotate(t, rows, sign):
            return (
                t * tab_c[rows, :]
                + sign * (pltpu.roll(t, 120, 1) * tab_a[rows, :])
                + sign * (pltpu.roll(t, 8, 1) * tab_b[rows, :])
            )

        @pl.loop(0, Z)
        def _(c):
            rows = blk(c, LOC)
            res = nn(attn_n[rows, :], wqkv[...])
            for p in range(PAIRS):
                lanes = slice(128 * p, 128 * p + 128)
                t = res[:, lanes] + qkv_b[0][:, lanes]
                q_s[rows, lanes] = (rotate(t, rows, 1.0) * 0.125).astype(BF)
                t = res[:, 256 + 128 * p : 384 + 128 * p] + qkv_b[1][:, lanes]
                k_s[rows, lanes] = rotate(t, rows, 1.0).astype(BF)
            v_s[rows, :] = (res[:, 512:] + qkv_b[2]).astype(BF)

        lane = lax.broadcasted_iota(jnp.int32, (QB, 128), 1)

        def twice(t):
            zero = jnp.zeros_like(t)
            return jnp.concatenate(
                [jnp.where(lane < HEAD, t, zero), jnp.where(lane >= HEAD, t, zero)], axis=0
            )

        def fold(t):
            return jnp.where(lane < HEAD, t[:QB], t[QB:])

        def window(i):
            first = pl.multiple_of(jnp.maximum(i * QB - (KB - QB), 0), QB)
            at = first + lax.broadcasted_iota(jnp.int32, (QB, KB), 1)
            row = i * QB + lax.broadcasted_iota(jnp.int32, (QB, KB), 0)
            ok = (at <= row) & (at >= start[blk(i, QB), :])
            bias = jnp.where(ok, 0.0, -1e30)
            return pl.ds(first, KB), jnp.concatenate([bias, bias], axis=0)

        @pl.loop(0, TOK // QB)
        def _(i):
            keys, bias = window(i)
            rows = blk(i, QB)
            for p in range(PAIRS):
                lanes = slice(128 * p, 128 * p + 128)
                s = nt(twice(q_s[rows, lanes]), k_s[keys, lanes]) + bias
                top = jnp.max(s, axis=1, keepdims=True)
                e = jnp.exp(s - top)
                total = jnp.sum(e, axis=1, keepdims=True)
                lse[p, blk(i, 2 * QB), :] = top + jnp.log(total)
                prob = (e * (1.0 / total)).astype(BF)
                ctx[rows, lanes] = fold(nn(prob, v_s[keys, lanes])).astype(BF)

        up_shift = upb[...]

        @pl.loop(0, Z)
        def _(c):
            h32[...] = nn(mlp_n[blk(c, LOC), :], wup[...])

            def act(i, carry):
                v = h32[blk(i, 16), :] + up_shift
                cdf = 0.5 + 0.5 * lax.erf(v * (0.5**0.5))
                rows = pl.ds(pl.multiple_of(c * LOC + i * 16, 16), 16)
                hidden[rows, :] = (v * cdf).astype(BF)
                dgelu[rows, :] = (
                    cdf + v * jnp.exp(-0.5 * v * v) * (1.0 / math.sqrt(2.0 * math.pi))
                ).astype(BF)
                return carry

            lax.fori_loop(0, LOC // 16, act, 0)

        gg.relay()

        @pl.loop(0, Z)
        def _(j):
            c = lax.rem(z + 1 + j, Z)
            rows = blk(c, LOC)
            res = nn(ctx[rows, :], wout[...]) + nn(hidden[rows, :], wdown[...])

            @pl.when(j < Z - 1)
            def _():
                part[rows, :] = res.astype(BF)

            @pl.when(j == Z - 1)
            def _():
                own[...] = res + x_in[...].astype(F32) + bias_o

    else:
        gg.relay()
    for c in near[1:]:
        gg.wait(c)

    class Scatter:
        def __init__(self, side):
            self.side = side
            self.v = recvs.take(Z)
            self.rv = recvs.take(1)
            self.recv = zrecv.at[pl.ds(side * TOK, TOK)]
            self.hold = zrelay.at[pl.ds(side * LOC, LOC)]

        def send(self):
            s = sends.take(1)
            go(part.at[blk(0, LOC)], self.hold, s, self.rv, (r, 2), z == 3)
            go(part.at[blk(3, LOC)], self.hold, s, self.rv, (r, 1), z == 0)
            for d in (2, -2, 1, -1):
                t = z + d
                ok = (t >= 0) & (t < Z)
                if abs(d) == 2:
                    ok = ok & ((z == 0) | (z == 3))
                self.one(t, ok)

        def one(self, t, ok):
            t = jnp.clip(t, 0, Z - 1)
            go(
                part.at[blk(t, LOC)],
                self.recv.at[blk(z, LOC)],
                sends.take(1),
                self.v + z,
                (r, t),
                ok,
            )

        def relay(self):
            mid = (z == 1) | (z == 2)
            t = jnp.where(z == 1, 3, 0)
            arrived(self.hold, self.rv, mid)

            @pl.when(mid)
            def _():
                def add(i, carry):
                    rows = pl.ds(pl.multiple_of(t * LOC + i * 16, 16), 16)
                    part[rows, :] = part[rows, :] + self.hold[blk(i, 16), :]
                    return carry

                lax.fori_loop(0, LOC // 16, add, 0, unroll=2)

            self.one(t, mid)

        def finish(self):
            for d in (1, -1, 2, -2):
                c = z + d
                ok = (c >= 0) & (c < Z)
                cc = jnp.clip(c, 0, Z - 1)
                arrived(self.recv.at[blk(cc, LOC)], self.v + cc, ok)

                @pl.when(ok)
                def _():
                    def add(i, carry):
                        rows = blk(i, 16)
                        got = self.recv[pl.ds(pl.multiple_of(cc * LOC + i * 16, 16), 16), :]
                        own[rows, :] += got.astype(F32)
                        return carry

                    lax.fori_loop(0, LOC // 16, add, 0, unroll=2)

    def flush():
        for copy, when in [p for p in pending if p is not None]:
            if when is None:
                copy.wait_send()
            else:
                pl.when(when)(copy.wait_send)
        pending.clear()

    if stage >= 3:
        s_out = Scatter(0)
        s_out.send()

        g_out[...] = tn(ctx[...], og_all[...]).astype(BF)

        @pl.loop(0, Z)
        def _(c):
            g_down[blk(c, 256), :] = tn(hidden[:, blk(c, 256)], og_all[...]).astype(BF)

        vsum[...] = jnp.zeros_like(vsum)

        @pl.loop(0, Z)
        def _(c):
            rows = blk(c, LOC)
            gctx[rows, :] = nt(og_all[rows, :], wout[...]).astype(BF)
            h32[...] = nt(og_all[rows, :], wdown[...])

            def act(i, carry):
                at = pl.ds(pl.multiple_of(c * LOC + i * 16, 16), 16)
                g = (h32[blk(i, 16), :] * dgelu[at, :].astype(F32)).astype(BF)
                dgelu[at, :] = g
                return carry + g.astype(F32)

            total = lax.fori_loop(0, LOC // 16, act, jnp.zeros((16, 1024), F32))
            vsum[pl.ds(7 + z, 1), :] += jnp.sum(total, axis=0, keepdims=True)

        dhid = dgelu
        s_out.relay()

        acc[...] = jnp.zeros_like(acc)
        dk[...] = jnp.zeros_like(dk)
        dv[...] = jnp.zeros_like(dv)

        @pl.loop(0, TOK // QB)
        def _(i):
            keys, bias = window(i)
            rows = blk(i, QB)
            for p in range(PAIRS):
                lanes = slice(128 * p, 128 * p + 128)
                q2 = twice(q_s[rows, lanes])
                kk = k_s[keys, lanes]
                g2 = twice(gctx[rows, lanes])
                s = nt(q2, kk) + bias
                prob = jnp.exp(s - lse[p, blk(i, 2 * QB), :])
                dp = nt(g2, v_s[keys, lanes])
                inner = jnp.sum(prob * dp, axis=1, keepdims=True)
                ds = (prob * (dp - inner)).astype(BF)
                dq[rows, lanes] = fold(nn(ds, kk)) * 0.125
                dk[keys, lanes] += tn(ds, q2)
                dv[keys, lanes] += tn(prob.astype(BF), g2)

        @pl.loop(0, Z)
        def _(c):
            rows = blk(c, LOC)
            for p in range(PAIRS):
                lanes = slice(128 * p, 128 * p + 128)
                dqkv[rows, lanes] = rotate(dq[rows, lanes], rows, -1.0).astype(BF)
                dqkv[rows, 256 + 128 * p : 384 + 128 * p] = rotate(
                    dk[rows, lanes], rows, -1.0
                ).astype(BF)
            dqkv[rows, 512:] = dv[rows, :].astype(BF)
            sums = jnp.sum(dqkv[rows, :].astype(F32), axis=0, keepdims=True)
            for s in range(3):
                vsum[4 + s : 5 + s, blk(z, 256)] += sums[:, 256 * s : 256 * s + 256]

        s_out.finish()
        outputs[...] = own[...].astype(BF)
        flush()

        @pl.loop(0, Z)
        def _(j):
            c = lax.rem(z + 1 + j, Z)
            rows = blk(c, LOC)
            g32[...] = nt(dqkv[rows, :], wqkv[...])
            h32[...] = nt(dhid[rows, :], wup[...])

            def back(i, carry):
                at = pl.ds(pl.multiple_of(c * LOC + i * 16, 16), 16)
                here = blk(i, 16)
                xhat = (x_all[at, :].astype(F32) - mean_s[at, :]) * rstd_s[at, :]
                ga, gm = g32[here, :], h32[here, :]
                for k, v in enumerate((ga * xhat, ga, gm * xhat, gm)):
                    acc[k] += v[:8] + v[8:]
                g32[here, :] = ga * gain_a + gm * gain_m
                return carry

            lax.fori_loop(0, LOC // 16, back, 0)

            @pl.when(j < Z - 1)
            def _():
                part[rows, :] = g32[...].astype(BF)

            @pl.when(j == Z - 1)
            def _():
                own[...] = g32[...]

        for k in range(4):
            vsum[k : k + 1, :] = jnp.sum(acc[k], axis=0, keepdims=True)
        s_in = Scatter(1)
        s_in.send()

        @pl.loop(0, Z)
        def _(c):
            g_qkv[c] = tn(attn_n[:, blk(c, 256)], dqkv[...]).astype(BF)
            g_up[c] = tn(mlp_n[:, blk(c, 256)], dhid[...]).astype(BF)

        s_in.relay()

        def add_og(i, carry):
            return carry + og_all[pl.ds(pl.multiple_of(z * LOC + i * 16, 16), 16), :].astype(F32)

        vsum[11:12, :] = jnp.sum(
            lax.fori_loop(0, LOC // 16, add_og, jnp.zeros((16, 1024), F32)), axis=0, keepdims=True
        )

    if stage >= 4:
        class Stream:
            def __init__(self, order, grad, temp, final, to_z=None):
                self.order, self.idx = order, index_of(order)
                self.grad, self.temp, self.final, self.to_z = grad, temp, final, to_z
                self.v = recvs.take(bits)
                self.g = recvs.take(nb)
                self.first, self.size, self.off = 0, chunks, 0

            def halve(self, k):
                if k < nb:
                    self.size //= 2
                    b = self.order[k]
                    mine = self.first + bit_of(r, b) * self.size
                    other = self.first + (1 - bit_of(r, b)) * self.size
                else:
                    b, mine, other = k, self.first, self.first
                self.mine = mine
                self.at = len(pending)
                go(
                    self.grad(other, self.size),
                    self.temp(self.off, self.size),
                    sends.take(1),
                    self.v + k,
                    (flip(r, b), z),
                )

            def add(self, k):
                got = self.temp(self.off, self.size)
                arrived(got, self.v + k)
                keep = self.grad(self.mine, self.size)
                if k >= nb:
                    pending[self.at][0].wait_send()
                    pending[self.at] = None
                n = keep.shape[-2] // 16
                for i in range(keep.shape[0] if len(keep.shape) == 3 else 1):
                    a, c = (keep.at[i], got.at[i]) if len(keep.shape) == 3 else (keep, got)

                    def step(j, carry):
                        a[blk(j, 16), :] = a[blk(j, 16), :] + c[blk(j, 16), :]
                        return carry

                    lax.fori_loop(0, n, step, 0)
                self.off += self.size
                self.first = self.mine

            def place(self):
                if self.to_z is None:
                    self.own = [local(self.grad(self.idx, 1), self.final(self.idx, 1))]
                    return
                self.zv = [recvs.take(Z) for _ in self.to_z]
                self.own = []
                for v, (src, dst) in zip(self.zv, self.to_z):
                    for step in (1, 3, 2):
                        t = lax.rem(z + step, Z)
                        go(src(t, self.idx), dst(z, self.idx), sends.take(1), v + z, (r, t))
                    self.own.append(local(src(z, self.idx), dst(z, self.idx)))

            def placed(self):
                if self.to_z is not None:
                    for v, (src, dst) in zip(self.zv, self.to_z):
                        for step in (1, 3, 2):
                            t = lax.rem(z + step, Z)
                            arrived(dst(t, self.idx), v + t)
                for copy in self.own:
                    copy.wait()

            def gather(self, k):
                size = 1 << k
                first = lax.div(self.idx, size) * size
                go(
                    self.final(first, size),
                    self.final(first, size),
                    sends.take(1),
                    self.g + k,
                    (flip(r, self.order[nb - 1 - k]), z),
                )

            def gathered(self, k):
                size = 1 << k
                first = flip(lax.div(self.idx, size), 0) * size
                arrived(self.final(first, size), self.g + k)

        def rows_of(ref, unit, lanes=slice(None)):
            def region(first, n):
                return ref.at[pl.ds(pl.multiple_of(first * unit, unit), n * unit), lanes]

            return region

        def deep_rows(ref):
            def region(first, n):
                return ref.at[:, pl.ds(pl.multiple_of(first * cr, cr), n * cr), :]

            return region

        def z_rows(ref, width, lanes):
            def src(t, idx):
                return ref.at[t, pl.ds(pl.multiple_of(idx * cr, cr), cr), lanes]

            return src

        def z_cols(ref, first, width):
            def dst(t, idx):
                return ref.at[
                    pl.ds(pl.multiple_of(idx * cr, cr), cr),
                    pl.ds(pl.multiple_of(first + t * width, width), width),
                ]

            return dst

        cd = FF // Z // chunks
        left, right = pl.ds(0, 512), pl.ds(512, 512)
        streams = [
            Stream(order_a, rows_of(g_down, cd, left), rows_of(t_down, cd, left), rows_of(f_down, cd, left)),
            Stream(order_b, rows_of(g_down, cd, right), rows_of(t_down, cd, right), rows_of(f_down, cd, right)),
            Stream(order_a, rows_of(g_out, cr), rows_of(t_out, cr), rows_of(f_out, cr)),
            Stream(
                order_b,
                deep_rows(g_up),
                deep_rows(t_up),
                rows_of(f_up, cr),
                [(z_rows(g_up, 1024, slice(None)), z_cols(f_up, 0, 1024))],
            ),
            Stream(
                order_a,
                deep_rows(g_qkv),
                deep_rows(t_qkv),
                rows_of(f_qkv, cr),
                [
                    (z_rows(g_qkv, 256, pl.ds(256 * s, 256)), z_cols(f_qkv, D * s, 256))
                    for s in range(3)
                ],
            ),
        ]
        vec_steps = [(0, b) for b in range(bits)] + [(1, b) for b in range(2)]
        vec_v2 = recvs.take(len(vec_steps))

        def vec_start(i):
            axis, b = vec_steps[i]
            dev = (flip(r, b), z) if axis == 0 else (r, flip(z, b))
            go(vsum, vrecv.at[i], sends.take(1), vec_v2 + i, dev)

        def vec_end(i):
            arrived(vrecv.at[i], vec_v2 + i)
            pending[-1][0].wait_send()
            pending.pop()
            vsum[...] = vsum[...] + vrecv[i]

        for k in range(bits):
            for s in streams:
                s.halve(k)
            for s in streams:
                s.add(k)
        s_in.finish()
        here = blk(z, LOC)

        def finish(i, carry):
            rows = blk(i, 16)
            at = pl.ds(pl.multiple_of(z * LOC + i * 16, 16), 16)
            rstd = rstd_s[at, :]
            xhat = (x_all[at, :].astype(F32) - mean_s[at, :]) * rstd
            g = own[rows, :]
            m1 = jnp.mean(g, axis=1, keepdims=True)
            m2 = jnp.mean(g * xhat, axis=1, keepdims=True)
            res = rstd * (g - m1 - xhat * m2)
            in_grad[rows, :] = (og_all[at, :].astype(F32) + res).astype(BF)
            return carry

        for s in streams:
            s.place()
        lax.fori_loop(0, LOC // 16, finish, 0)
        for s in streams:
            s.placed()
        for k in range(nb):
            for s in streams:
                s.gather(k)
            for s in streams:
                s.gathered(k)
        flush()
        for i in range(len(vec_steps)):
            vec_start(i)
            vec_end(i)
        vec_out[...] = vsum[...]

    flush()


def shards(
    replicas,
    stage,
    inputs,
    out_grad,
    segment_ids,
    ln_gain_attn,
    ln_bias_attn,
    ln_gain_mlp,
    ln_bias_mlp,
    qkv_weight,
    qkv_bias,
    out_weight,
    up_weight,
    up_bias,
    down_weight,
    output_bias,
    probe=(),
):
    z = lax.axis_index("shard")
    seg = segment_ids[0]
    count0 = jnp.sum((seg == 0).astype(jnp.int32))
    count1 = jnp.sum((seg <= 1).astype(jnp.int32))
    start = jnp.where(seg == 0, 0, jnp.where(seg == 1, count0, count1))
    position = (jnp.arange(TOK, dtype=jnp.int32) - start).astype(F32)
    half = ROT // 2
    freq = 1.0 / 10000.0 ** (jnp.arange(half, dtype=F32) * 2.0 / ROT)
    angles = position[:, None] * freq
    cosine, sine = jnp.cos(angles), jnp.sin(angles)
    pad1 = jnp.ones((TOK, HEAD - ROT), F32)
    pad0 = jnp.zeros((TOK, HEAD - ROT), F32)
    none = jnp.zeros((TOK, half), F32)
    tab_c = jnp.tile(jnp.concatenate([cosine, cosine, pad1], axis=1), (1, 2))
    tab_a = jnp.tile(jnp.concatenate([-sine, none, pad0], axis=1), (1, 2))
    tab_b = jnp.tile(jnp.concatenate([none, sine, pad0], axis=1), (1, 2))
    vec = jnp.concatenate(
        [
            ln_gain_attn,
            ln_bias_attn,
            ln_gain_mlp,
            ln_bias_mlp,
            qkv_bias,
            output_bias,
            jnp.zeros((8 * 256,), BF),
        ]
    ).reshape(16, 256)
    upb = up_bias.astype(F32).reshape(1, 1024)

    bits = int(math.log2(replicas))
    vm = pl.BlockSpec(memory_space=pltpu.VMEM)
    hbm = pl.BlockSpec(memory_space=pl.ANY)

    def v(*shape, dtype=BF):
        return pltpu.VMEM(shape, dtype)

    scratch = dict(
        x_all=v(TOK, D),
        og_all=v(TOK, D),
        vec_all=v(64, 256),
        wqkv=v(D, 768),
        wup=v(D, 1024),
        wout=v(256, D),
        wdown=v(1024, D),
        attn_n=v(TOK, D),
        mlp_n=v(TOK, D),
        mean_s=v(TOK, 1, dtype=F32),
        rstd_s=v(TOK, 1, dtype=F32),
        q_s=v(TOK, 256),
        k_s=v(TOK, 256),
        v_s=v(TOK, 256),
        ctx=v(TOK, 256),
        lse=v(PAIRS, 2 * TOK, 1, dtype=F32),
        h32=v(LOC, 1024, dtype=F32),
        g32=v(LOC, 1024, dtype=F32),
        acc=v(4, 8, 1024, dtype=F32),
        hidden=v(TOK, 1024),
        dgelu=v(TOK, 1024),
        part=v(TOK, D),
        own=v(LOC, D, dtype=F32),
        zrecv=v(2 * TOK, D),
        zrelay=v(2 * LOC, D),
        gctx=v(TOK, 256),
        dq=v(TOK, 256, dtype=F32),
        dk=v(TOK, 256, dtype=F32),
        dv=v(TOK, 256, dtype=F32),
        dqkv=v(TOK, 768),
        g_qkv=v(Z, 256, 768),
        g_up=v(Z, 256, 1024),
        g_out=v(256, D),
        g_down=v(1024, D),
        t_qkv=v(Z, 256, 768),
        t_up=v(Z, 256, 1024),
        t_out=v(256, D),
        t_down=v(1024, D),
        vsum=v(16, 1024, dtype=F32),
        vrecv=v(bits + 2, 16, 1024, dtype=F32),
        ssem=pltpu.SemaphoreType.DMA((NSEM,)),
        rsem=pltpu.SemaphoreType.DMA((NSEM,)),
        lsem=pltpu.SemaphoreType.DMA((32,)),
    )
    out_shape = [
        jax.ShapeDtypeStruct((LOC, D), BF),
        jax.ShapeDtypeStruct((LOC, D), BF),
        jax.ShapeDtypeStruct((256, 3 * D), BF),
        jax.ShapeDtypeStruct((256, FF), BF),
        jax.ShapeDtypeStruct((256, D), BF),
        jax.ShapeDtypeStruct((1024, D), BF),
        jax.ShapeDtypeStruct((16, 1024), F32),
    ]
    out_specs = [vm, vm, hbm, hbm, hbm, hbm, vm]
    names = list(scratch)
    extra = [jax.ShapeDtypeStruct(scratch[n].shape, scratch[n].dtype) for n in probe]

    def body(*refs):
        ins, rest = refs[:12], refs[12:]
        outs, rest = rest[: len(out_shape)], rest[len(out_shape) :]
        dumps, held = rest[: len(extra)], rest[len(extra) :]
        layer(replicas, stage, *ins, *outs, **dict(zip(names, held)))
        if probe:

            def run(sem):
                for n, d in zip(probe, dumps):
                    copy = pltpu.make_async_copy(held[names.index(n)], d, sem)
                    copy.start()
                    copy.wait()

            pl.run_scoped(run, pltpu.SemaphoreType.DMA)

    res = pl.pallas_call(
        body,
        out_shape=out_shape + extra,
        in_specs=[vm] + [hbm] * 6 + [vm] * 5,
        out_specs=out_specs + [hbm] * len(extra),
        scratch_shapes=list(scratch.values()),
        compiler_params=pltpu.CompilerParams(
            collective_id=0,
            has_side_effects=True,
            vmem_limit_bytes=62 * 2**20,
        ),
    )(
        inputs.reshape(LOC, D),
        out_grad.reshape(LOC, D),
        qkv_weight,
        up_weight,
        out_weight,
        down_weight,
        vec,
        upb,
        start.reshape(TOK, 1),
        tab_c,
        tab_a,
        tab_b,
    )
    outputs, in_grad, f_qkv, f_up, f_out, f_down, vec_out = res[:7]

    def cut(first, n):
        return lax.dynamic_slice_in_dim(first, z * n, n, 0)

    final = (
        outputs.reshape(1, LOC, D),
        in_grad.reshape(1, LOC, D),
        cut(vec_out[0], 256),
        cut(vec_out[1], 256),
        cut(vec_out[2], 256),
        cut(vec_out[3], 256),
        f_qkv.astype(F32),
        cut(vec_out[4:7].reshape(3072), 768),
        f_out.astype(F32),
        f_up.astype(F32),
        cut(vec_out[7:11].reshape(4096), 1024),
        f_down.astype(F32),
        cut(vec_out[11], 256),
    )
    return final + tuple(r[None, None] for r in res[7:]) if probe else final


def solution(mesh, stage=STAGE, probe=()):
    seq = P("replica", "shard", None)
    row = P("shard", None)
    one = P("shard")
    return jax.shard_map(
        partial(shards, mesh.shape["replica"], stage, probe=probe),
        mesh=mesh,
        in_specs=(seq, seq, P("replica", None), one, one, one, one, row, one, row, row, one, row, one),
        out_specs=(seq, seq, one, one, one, one, row, one, row, row, one, row, one)
        + tuple(P("replica", "shard") for _ in probe),
        check_vma=False,
    )
```

time: 1790 us -> 269 us (0.15)
  waiting for transfers between devices: 1440 us -> 0 us
  Pallas kernels: 0 us -> 238 us
  matrix products: 126 us -> 0 us
  blocking collectives: 120 us -> 0 us
  local copies, waits for them, and re-layouts: 55.4 us -> 14.5 us
    reduce_scatter x6 -> x0, waiting for transfers between devices: 955 us -> none  [the longest x1 283 us: shards(): lax.psum_scatter(grad_down_weight, 'shard', scatter_dimension=0, tiled=True)]
    all_gather x6 -> x0, waiting for transfers between devices: 378 us -> none  [the longest x1 135 us: shards(): lax.all_gather(up_weight, 'shard', axis=0, tiled=True)]
    pallas_call x0 -> x1, Pallas kernels: none -> 238 us  [shards(): pl.pallas_call(body, out_shape=out_shape + extra, in_specs=[vm] + [hbm] *...]
    dot_general x18 -> x0, matrix products: 126 us -> none  [the longest x1 15.8 us: shards(): up_sum = jnp.dot(mlp_normed, pieces[1], preferred_element_type=jnp.float32)]
    psum x1 -> x0, waiting for transfers between devices: 101 us -> none  [shards(): lax.psum((in_shares[0], in_shares[1], in_shares[2], in_shares[3], in_shar...]
    all_gather x7 -> x0, blocking collectives: 79.3 us -> none  [the longest x1 14.7 us: shards(): lax.all_gather(qkv_bias, 'shard', axis=0, tiled=True)]
    unnamed x116 -> x36, local copies, waits for them, and re-layouts: 30.6 us -> 3.75 us
    psum x1 -> x0, blocking collectives: 23.6 us -> none  [shards(): lax.psum((in_shares[0], in_shares[1], in_shares[2], in_shares[3], in_shar...]
  transfers between devices with their start and end apart: 13 -> 0, of which waited for: 13 -> 0; matrix products, arithmetic and copies ran while one was open for 10% -> 0% of each run, Pallas kernels for 0% -> 0%
where the time goes in v1:
time: 269 us
  Pallas kernels  238 us (88%)
  other arithmetic  15.4 us (6%)
  local copies, waits for them, and re-layouts  14.5 us (5%)
    pallas_call x1, Pallas kernels, shards(): pl.pallas_call(body, out_shape=out_shape + extra, in_specs=[vm] + [hbm] *...  238 us

profile of v1, /device:TPU:0, one launch (start us, length us, event | category | flops | bytes accessed | tf_op | source)
XLA Modules:
  0.0 268.7 jit_solution(15957025778465119261)
XLA Ops:
  0.6 1.3 fusion.1
  2.0 2.0 compare_select_fusion.1
  4.0 0.2 multiply_sine_fusion
  4.5 1.0 copy.28.refs_9_
  5.6 1.0 copy.29.refs_10_
  6.7 1.0 copy.30.refs_11_
  7.7 1.3 fusion.4
  9.0 1.0 copy.27.refs_8_
  10.2 0.2 dynamic-update-slice.1
  10.4 0.2 dynamic-update-slice.2
  10.7 0.2 dynamic-update-slice.3
  10.9 0.2 dynamic-update-slice.4
  11.1 0.2 dynamic-update-slice.5
  11.3 0.6 reshape.135.refs_6_
  11.9 0.6 reshape.142
  12.5 238.0 %shard_map.237 = (bf16[256,1024]{1,0:T(8,128)(2,1)}, bf16[256,1024]{1,0:T(8,128)(2,1)}, bf16[256,3072]{1,0:T(8,128)(2,1)}, bf16[256,4096]{1,0:T(8,128)(2,1)}, bf...) custom-call(bf16[256,1024]{1,0:T(8,128)(2,1)} %bitcast.24, bf16[256,1024]{1,0:T(8,128)(2,1)} %bitcast.25, ...), custom_call_target="tpu_custom_call" | custom-call | tf_op jit(solution)/shard_map/pallas_call | solution.py:942
  250.6 0.9 fusion.3
  251.5 0.6 constant_dynamic-slice_fusion.4
  252.1 0.6 constant_dynamic-slice_fusion.3
  252.6 0.6 constant_dynamic-slice_fusion.2
  253.2 0.6 constant_dynamic-slice_fusion.1
  253.8 0.6 constant_dynamic-slice_fusion
  254.3 0.8 slice_bitcast_fusion
  255.2 0.6 dynamic_slice.40
  255.8 0.8 slice.25
  256.6 0.7 dynamic_slice.39
  257.2 4.2 %convert_element_type.33 = f32[256,4096]{1,0:T(8,128)} convert(bf16[256,4096]{1,0:T(8,128)(2,1)} %get-tuple-element.25) | non-fusion elementwise | flops 1048576 | bytes 6291456 | tf_op jit(solution)/shard_map/convert_element_type | solution.py:982
  261.5 2.5 convert_element_type.34
  264.0 2.0 convert_element_type.31
  266.0 1.1 convert_element_type.32
  267.1 0.8 copy.43
  267.9 0.8 copy.44
  (42 shorter events, 0.7 us)
Async XLA Ops:
  5.5 2.2 copy-start.5
  5.5 4.5 %copy-start.8 = (bf16[256]{0:T(256)(128)(2,1)S(1)}, bf16[256]{0:T(256)(128)(2,1)}, u32[]{:S(2)}) copy-start(bf16[256]{0:T(256)(128)(2,1)} %param.17) | copy-start | bytes 1540
  5.5 4.7 %copy-start.9 = (bf16[256]{0:T(256)(128)(2,1)S(1)}, bf16[256]{0:T(256)(128)(2,1)}, u32[]{:S(2)}) copy-start(bf16[256]{0:T(256)(128)(2,1)} %param.18) | copy-start | bytes 1540
  5.5 4.9 %copy-start.10 = (bf16[256]{0:T(256)(128)(2,1)S(1)}, bf16[256]{0:T(256)(128)(2,1)}, u32[]{:S(2)}) copy-start(bf16[256]{0:T(256)(128)(2,1)} %param.19) | copy-start | bytes 1540
  5.5 5.1 %copy-start.11 = (bf16[256]{0:T(256)(128)(2,1)S(1)}, bf16[256]{0:T(256)(128)(2,1)}, u32[]{:S(2)}) copy-start(bf16[256]{0:T(256)(128)(2,1)} %param.20) | copy-start | bytes 1540
  5.6 5.3 %copy-start.7 = (bf16[768]{0:T(1024)(128)(2,1)S(1)}, bf16[768]{0:T(1024)(128)(2,1)}, u32[]{:S(2)}) copy-start(bf16[768]{0:T(1024)(128)(2,1)} %param.22) | copy-start | bytes 4612
  5.6 5.5 %copy-start.12 = (bf16[256]{0:T(256)(128)(2,1)S(1)}, bf16[256]{0:T(256)(128)(2,1)}, u32[]{:S(2)}) copy-start(bf16[256]{0:T(256)(128)(2,1)} %param.27) | copy-start | bytes 1540
  5.6 6.3 %copy-start.6 = (bf16[1024]{0:T(1024)(128)(2,1)S(1)}, bf16[1024]{0:T(1024)(128)(2,1)}, u32[]{:S(2)}) copy-start(bf16[1024]{0:T(1024)(128)(2,1)} %param.25) | copy-start | bytes 6148
  257.2 4.3 %copy-start = (bf16[1024,1024]{1,0:T(8,128)(2,1)S(1)}, bf16[1024,1024]{1,0:T(8,128)(2,1)}, u32[]{:S(2)}) copy-start(bf16[1024,1024]{1,0:T(8,128)(2,1)} %get-tuple-element.26) | copy-start | bytes 6291460
  261.5 2.5 copy-start.1
  264.0 2.0 copy-start.2
  264.0 3.1 %copy-start.4 = (bf16[256,1024]{1,0:T(8,128)(2,1)S(1)}, bf16[256,1024]{1,0:T(8,128)(2,1)}, u32[]{:S(2)}) copy-start(bf16[256,1024]{1,0:T(8,128)(2,1)} %get-tuple-element.20) | copy-start | bytes 1572868
  266.0 1.9 copy-start.3

commit v2 on v1

v2 whole, which is shorter than its diff:
```python
import math
from functools import partial

import jax
import jax.numpy as jnp
from jax import lax
from jax.experimental import pallas as pl
from jax.experimental.pallas import tpu as pltpu
from jax.sharding import PartitionSpec as P

D = 1024
FF = 4096
HEADS = 16
HEAD = 64
ROT = 16
Z = 4
LOC = 256
TOK = 1024
PAIRS = 2
QB = 128
KB = 640
EPS = 1e-05
BF = jnp.bfloat16
F32 = jnp.float32
MESH = pl.DeviceIdType.MESH
NSEM = 256
SUB = 2


def bit_of(value, place):
    return lax.rem(lax.div(value, 1 << place), 2)


def flip(value, place):
    return value + (1 - 2 * bit_of(value, place)) * (1 << place)


def nn(a, b):
    return jnp.dot(a, b, preferred_element_type=F32)


def nt(a, b):
    return lax.dot_general(a, b, (((1,), (1,)), ((), ())), preferred_element_type=F32)


def tn(a, b):
    return lax.dot_general(a, b, (((0,), (0,)), ((), ())), preferred_element_type=F32)


def blk(i, n):
    return pl.ds(pl.multiple_of(i * n, n), n)


class Count:
    def __init__(self):
        self.used = 0

    def take(self, n):
        first = self.used
        self.used += n
        assert self.used <= NSEM
        return first


def layer(
    replicas,
    x_in,
    og_in,
    qkv_w,
    up_w,
    out_w,
    down_w,
    vec_in,
    tab_in,
    outputs,
    in_grad,
    f_qkv,
    f_up,
    f_out,
    f_down,
    vec_out,
    x_all,
    og_all,
    vec_all,
    tab,
    tab_c,
    tab_a,
    tab_b,
    start,
    wqkv,
    wup,
    wout,
    wdown,
    attn_n,
    mlp_n,
    mean_s,
    rstd_s,
    q_s,
    k_s,
    v_s,
    ctx,
    lse,
    h32,
    g32,
    acc,
    hidden,
    dgelu,
    part_o,
    part_i,
    own_o,
    own_i,
    land_o,
    land_i,
    gctx,
    dq,
    dk,
    dv,
    dqkv,
    g_qkv,
    g_up,
    g_out,
    g_down,
    t_qkv,
    t_up,
    t_out,
    t_down,
    vsum,
    vrecv,
    ssem,
    rsem,
    lsem,
):
    r = lax.axis_index("replica")
    z = lax.axis_index("shard")
    bits = int(math.log2(replicas))
    nb = min(bits, 4)
    chunks = 1 << nb
    sends, recvs, locals_ = Count(), Count(), Count()
    pending = []

    middle = (z == 1) | (z == 2)
    ends = (z == 0) | (z == 3)
    low = z < 2
    end = jnp.where(low, 0, 3)
    mid = jnp.where(low, 1, 2)
    other = 3 - mid
    far = 3 - end
    beside = z + 1 - 2 * lax.rem(z, 2)
    c1, c2, c3 = beside, other, far
    own_rows = blk(z, LOC)

    def remote(src, dst, s, v, dev):
        return pltpu.make_async_remote_copy(
            src_ref=src,
            dst_ref=dst,
            send_sem=ssem.at[s],
            recv_sem=rsem.at[v],
            device_id=dev,
            device_id_type=MESH,
        )

    def go(src, dst, s, v, dev, when=None):
        copy = remote(src, dst, s, v, dev)
        if when is None:
            copy.start()
        else:
            pl.when(when)(copy.start)
        pending.append((copy, when))

    def arrived(dst, v, when=None):
        copy = remote(dst, dst, 0, v, (r, z))
        if when is None:
            copy.wait_recv()
        else:
            pl.when(when)(copy.wait_recv)

    def local(src, dst):
        copy = pltpu.make_async_copy(src, dst, lsem.at[locals_.take(1)])
        copy.start()
        return copy

    def rows_at(first, n):
        return pl.ds(pl.multiple_of(first, n), n)

    vec_own = local(vec_in, vec_all.at[blk(z, 16)])
    tab_own = local(tab_in, tab)
    x_own = local(x_in, x_all.at[own_rows])

    barrier = pltpu.get_barrier_semaphore()
    for step in range(1, Z):
        pl.semaphore_signal(
            barrier, inc=1, device_id=(r, lax.rem(z + step, Z)), device_id_type=MESH
        )
    for b in range(bits):
        pl.semaphore_signal(barrier, inc=1, device_id=(flip(r, b), z), device_id_type=MESH)
    pl.semaphore_wait(barrier, Z - 1 + bits)

    order_a = list(range(nb))
    order_b = [0, *reversed(range(1, nb))]

    def index_of(order):
        return sum(bit_of(r, b) * (1 << (nb - 1 - k)) for k, b in enumerate(order))

    idx_a, idx_b = index_of(order_a), index_of(order_b)
    cr = LOC // chunks

    up_v, qkv_v, vec_v = recvs.take(Z), recvs.take(3 * Z), recvs.take(Z)
    for step in (1, 3, 2):
        t = lax.rem(z + step, Z)
        go(vec_in, vec_all.at[blk(z, 16)], sends.take(1), vec_v + z, (r, t))
    for step in (1, 3, 2):
        t = lax.rem(z + step, Z)
        go(
            up_w.at[blk(idx_a, cr), blk(t, 1024)],
            wup.at[rows_at(z * LOC + idx_a * cr, cr)],
            sends.take(1),
            up_v + z,
            (r, t),
        )
        for s in range(3):
            go(
                qkv_w.at[blk(idx_b, cr), rows_at(s * D + t * 256, 256)],
                wqkv.at[rows_at(z * LOC + idx_b * cr, cr), pl.ds(s * 256, 256)],
                sends.take(1),
                qkv_v + z * 3 + s,
                (r, t),
            )

    piece = LOC // SUB

    class Gather:
        def __init__(self, src, buf):
            self.src, self.buf = src, buf
            self.v = recvs.take(Z * SUB)

        def rows(self, c, k):
            return self.buf.at[rows_at(c * LOC + k * piece, piece)]

        def send(self):
            for k in range(SUB):
                for dev, when in ((mid, ends), (end, middle), (other, middle)):
                    go(
                        self.src.at[pl.ds(k * piece, piece)],
                        self.rows(z, k),
                        sends.take(1),
                        self.v + z * SUB + k,
                        (r, dev),
                        when,
                    )

        def hand(self, c, dev):
            for k in range(SUB):
                arrived(self.rows(c, k), self.v + c * SUB + k, middle)
                go(
                    self.rows(c, k),
                    self.rows(c, k),
                    sends.take(1),
                    self.v + c * SUB + k,
                    (r, dev),
                    middle,
                )

        def wait(self, c):
            for k in range(SUB):
                arrived(self.rows(c, k), self.v + c * SUB + k, ends)

    gx, gg = Gather(x_in, x_all), Gather(og_in, og_all)
    gx.send()
    own_up = local(up_w.at[:, blk(z, 1024)], wup.at[own_rows])
    own_qkv = [
        local(qkv_w.at[:, rows_at(s * D + z * 256, 256)], wqkv.at[own_rows, pl.ds(s * 256, 256)])
        for s in range(3)
    ]
    og_own = local(og_in, og_all.at[own_rows])
    w_own = [local(out_w, wout), local(down_w, wdown)]

    ag_v = recvs.take(3 * 2 * nb)

    def weight_region(kind, zz, first, n):
        ref = wup if kind == 0 else wqkv
        return ref.at[pl.ds(pl.multiple_of(zz * LOC + first * cr, cr), n * cr)]

    def weight_step(k):
        for j in range(1, Z):
            zz = lax.rem(z + j, Z)
            for kind, order, idx in ((0, order_a, idx_a), (1, order_b, idx_b)):
                b = order[nb - 1 - k]
                size = 1 << k
                first = lax.div(idx, size) * size
                go(
                    weight_region(kind, zz, first, size),
                    weight_region(kind, zz, first, size),
                    sends.take(1),
                    ag_v + ((j - 1) * 2 + kind) * nb + k,
                    (flip(r, b), z),
                )

    def weight_wait(k):
        for j in range(1, Z):
            zz = lax.rem(z + j, Z)
            for kind, idx in ((0, idx_a), (1, idx_b)):
                size = 1 << k
                first = flip(lax.div(idx, size), 0) * size
                arrived(weight_region(kind, zz, first, size), ag_v + ((j - 1) * 2 + kind) * nb + k)

    tab_own.wait()
    vec_own.wait()
    x_own.wait()
    own_up.wait()
    og_own.wait()
    for copy in own_qkv + w_own:
        copy.wait()
    lane = lax.broadcasted_iota(jnp.int32, (QB, 128), 1)
    turned = lax.rem(lane, HEAD) < ROT

    @pl.loop(0, TOK // 128)
    def _(i):
        at = blk(i, 128)
        cosine, sine, first = tab[0:8, at], tab[8:16, at], tab[16:24, at]
        none = jnp.zeros_like(cosine)
        half = [cosine, cosine, -sine, none, none, sine, first, none]
        wide = jnp.concatenate(half + half, axis=0).T
        tab_c[at, :] = jnp.where(turned, wide, 1.0)
        tab_a[at, :] = jnp.where(turned, pltpu.roll(wide, 112, 1), 0.0)
        tab_b[at, :] = jnp.where(turned, pltpu.roll(wide, 96, 1), 0.0)
        start[at, :] = wide[:, 48:49]

    for j in range(1, Z):
        zz = lax.rem(z + j, Z)
        arrived(vec_all.at[blk(zz, 16)], vec_v + zz)

    def vector(row):
        return jnp.concatenate(
            [vec_all[16 * c : 16 * c + 16, :][row : row + 1, :] for c in range(Z)], axis=1
        ).astype(F32)

    def vector256(i):
        block = vec_all[blk(lax.div(i, 3), 16), :].astype(F32)
        rows = lax.broadcasted_iota(jnp.int32, (16, 256), 0)
        return jnp.sum(jnp.where(rows == 4 + lax.rem(i, 3), block, 0.0), axis=0, keepdims=True)

    gain_a, bias_a, gain_m, bias_m, bias_o = [vector(i) for i in (0, 1, 2, 3, 7)]
    qkv_b = [vector256(s * Z + z) for s in range(3)]
    mine = vec_all[blk(z, 16), :]
    up_shift = jnp.concatenate([mine[8 + i : 9 + i, :] for i in range(4)], axis=1).astype(F32)

    def norm_rows(c):
        def norm(i, carry):
            rows = rows_at(c * LOC + i * 16, 16)
            v = x_all[rows, :].astype(F32)
            mean = jnp.mean(v, axis=1, keepdims=True)
            cen = v - mean
            rstd = lax.rsqrt(jnp.mean(cen * cen, axis=1, keepdims=True) + EPS)
            xhat = cen * rstd
            attn_n[rows, :] = (xhat * gain_a + bias_a).astype(BF)
            mlp_n[rows, :] = (xhat * gain_m + bias_m).astype(BF)
            mean_s[rows, :] = mean
            rstd_s[rows, :] = rstd
            return carry

        lax.fori_loop(0, LOC // 16, norm, 0, unroll=2)

    def rotate(t, rows, sign):
        return (
            t * tab_c[rows, :]
            + sign * (pltpu.roll(t, 120, 1) * tab_a[rows, :])
            + sign * (pltpu.roll(t, 8, 1) * tab_b[rows, :])
        )

    def project(c):
        rows = blk(c, LOC)
        res = nn(attn_n[rows, :], wqkv[...])
        for p in range(PAIRS):
            lanes = slice(128 * p, 128 * p + 128)
            t = res[:, lanes] + qkv_b[0][:, lanes]
            q_s[rows, lanes] = (rotate(t, rows, 1.0) * 0.125).astype(BF)
            t = res[:, 256 + 128 * p : 384 + 128 * p] + qkv_b[1][:, lanes]
            k_s[rows, lanes] = rotate(t, rows, 1.0).astype(BF)
        v_s[rows, :] = (res[:, 512:] + qkv_b[2]).astype(BF)
        h32[...] = nn(mlp_n[rows, :], wup[...])

        def act(i, carry):
            v = h32[blk(i, 16), :] + up_shift
            cdf = 0.5 + 0.5 * lax.erf(v * (0.5**0.5))
            at = rows_at(c * LOC + i * 16, 16)
            hidden[at, :] = (v * cdf).astype(BF)
            dgelu[at, :] = (
                cdf + v * jnp.exp(-0.5 * v * v) * (1.0 / math.sqrt(2.0 * math.pi))
            ).astype(BF)
            return carry

        lax.fori_loop(0, LOC // 16, act, 0)

    def twice(t):
        zero = jnp.zeros_like(t)
        return jnp.concatenate(
            [jnp.where(lane < HEAD, t, zero), jnp.where(lane >= HEAD, t, zero)], axis=0
        )

    def fold(t):
        return jnp.where(lane < HEAD, t[:QB], t[QB:])

    def window(i):
        first = pl.multiple_of(jnp.maximum(i * QB - (KB - QB), 0), QB)
        at = first + lax.broadcasted_iota(jnp.int32, (QB, KB), 1)
        row = i * QB + lax.broadcasted_iota(jnp.int32, (QB, KB), 0)
        ok = (at <= row) & (at.astype(F32) >= start[blk(i, QB), :])
        bias = jnp.where(ok, 0.0, -1e30)
        return pl.ds(first, KB), jnp.concatenate([bias, bias], axis=0)

    def attend(c):
        @pl.loop(0, LOC // QB)
        def _(j):
            i = c * (LOC // QB) + j
            keys, bias = window(i)
            rows = blk(i, QB)
            for p in range(PAIRS):
                lanes = slice(128 * p, 128 * p + 128)
                s = nt(twice(q_s[rows, lanes]), k_s[keys, lanes]) + bias
                top = jnp.max(s, axis=1, keepdims=True)
                e = jnp.exp(s - top)
                total = jnp.sum(e, axis=1, keepdims=True)
                lse[p, blk(i, 2 * QB), :] = top + jnp.log(total)
                prob = (e * (1.0 / total)).astype(BF)
                ctx[rows, lanes] = fold(nn(prob, v_s[keys, lanes])).astype(BF)

    class Scatter:
        def __init__(self, part, own, land):
            self.part, self.own, self.land = part, own, land
            self.v = recvs.take(5 * SUB)

        def slot(self, s, k):
            return self.land.at[rows_at(s * LOC + k * piece, piece)]

        def rows(self, c, k):
            return self.part.at[rows_at(c * LOC + k * piece, piece)]

        def send(self, c):
            place = jnp.clip(jnp.where(low, 3 - c, c), 0, 2)
            when = ends & (c != z)
            for k in range(SUB):
                go(
                    self.rows(c, k),
                    self.slot(place, k),
                    sends.take(1),
                    self.v + place * SUB + k,
                    (r, mid),
                    when,
                )

        def pass_on(self, came, c, dev, goes, when):
            for k in range(SUB):
                arrived(self.slot(came, k), self.v + came * SUB + k, when)

                @pl.when(when)
                def _():
                    def add(i, carry):
                        at = rows_at(c * LOC + k * piece + i * 16, 16)
                        got = rows_at(came * LOC + k * piece + i * 16, 16)
                        self.part[at, :] = self.part[at, :] + self.land[got, :]
                        return carry

                    lax.fori_loop(0, piece // 16, add, 0, unroll=2)

                go(
                    self.rows(c, k),
                    self.slot(goes, k),
                    sends.take(1),
                    self.v + goes * SUB + k,
                    (r, dev),
                    when,
                )

        def pass_far(self, when):
            self.pass_on(0, far, other, 3, when)

        def pass_other(self, when):
            self.pass_on(1, other, other, 4, when)

        def pass_end(self, when):
            self.pass_on(3, end, end, 0, when)

        def finish(self):
            for came, when in ((0, ends), (2, middle), (4, middle)):
                for k in range(SUB):
                    arrived(self.slot(came, k), self.v + came * SUB + k, when)

                @pl.when(when)
                def _():
                    def add(i, carry):
                        got = self.land[rows_at(came * LOC + i * 16, 16), :]
                        self.own[blk(i, 16), :] += got.astype(F32)
                        return carry

                    lax.fori_loop(0, LOC // 16, add, 0, unroll=2)

    s_out = Scatter(part_o, own_o, land_o)
    s_in = Scatter(part_i, own_i, land_i)

    def mix(c):
        rows = blk(c, LOC)
        res = nn(ctx[rows, :], wout[...]) + nn(hidden[rows, :], wdown[...])
        if c is z:
            own_o[...] = res + x_all[own_rows, :].astype(F32) + bias_o
        else:
            part_o[rows, :] = res.astype(BF)
            s_out.send(c)

    vsum[...] = jnp.zeros_like(vsum)
    acc[...] = jnp.zeros_like(acc)
    dk[...] = jnp.zeros_like(dk)
    dv[...] = jnp.zeros_like(dv)

    def side(c):
        rows = blk(c, LOC)
        gctx[rows, :] = nt(og_all[rows, :], wout[...]).astype(BF)
        h32[...] = nt(og_all[rows, :], wdown[...])

        def act(i, carry):
            at = rows_at(c * LOC + i * 16, 16)
            g = (h32[blk(i, 16), :] * dgelu[at, :].astype(F32)).astype(BF)
            dgelu[at, :] = g
            return carry + g.astype(F32)

        total = lax.fori_loop(0, LOC // 16, act, jnp.zeros((16, 1024), F32))
        vsum[pl.ds(7 + z, 1), :] += jnp.sum(total, axis=0, keepdims=True)

    dhid = dgelu

    def back(c):
        @pl.loop(0, LOC // QB)
        def _(j):
            i = c * (LOC // QB) + j
            keys, bias = window(i)
            rows = blk(i, QB)
            for p in range(PAIRS):
                lanes = slice(128 * p, 128 * p + 128)
                q2 = twice(q_s[rows, lanes])
                kk = k_s[keys, lanes]
                g2 = twice(gctx[rows, lanes])
                s = nt(q2, kk) + bias
                prob = jnp.exp(s - lse[p, blk(i, 2 * QB), :])
                dp = nt(g2, v_s[keys, lanes])
                inner = jnp.sum(prob * dp, axis=1, keepdims=True)
                ds = (prob * (dp - inner)).astype(BF)
                dq[rows, lanes] = fold(nn(ds, kk)) * 0.125
                dk[keys, lanes] += tn(ds, q2)
                dv[keys, lanes] += tn(prob.astype(BF), g2)

        rows = blk(c, LOC)
        for p in range(PAIRS):
            lanes = slice(128 * p, 128 * p + 128)
            dqkv[rows, lanes] = rotate(dq[rows, lanes], rows, -1.0).astype(BF)
            dqkv[rows, 256 + 128 * p : 384 + 128 * p] = rotate(dk[rows, lanes], rows, -1.0).astype(BF)
        dqkv[rows, 512:] = dv[rows, :].astype(BF)
        sums = jnp.sum(dqkv[rows, :].astype(F32), axis=0, keepdims=True)
        for s in range(3):
            vsum[4 + s : 5 + s, blk(z, 256)] += sums[:, 256 * s : 256 * s + 256]
        g32[...] = nt(dqkv[rows, :], wqkv[...])
        h32[...] = nt(dhid[rows, :], wup[...])

        def step(i, carry):
            at = rows_at(c * LOC + i * 16, 16)
            here = blk(i, 16)
            xhat = (x_all[at, :].astype(F32) - mean_s[at, :]) * rstd_s[at, :]
            ga, gm = g32[here, :], h32[here, :]
            for k, v in enumerate((ga * xhat, ga, gm * xhat, gm)):
                acc[k] += v[:8] + v[8:]
            g = ga * gain_a + gm * gain_m
            g32[here, :] = g
            part_i[at, :] = g.astype(BF)
            return carry

        lax.fori_loop(0, LOC // 16, step, 0)

        @pl.when(z == c)
        def _():
            own_i[...] = g32[...]

        s_in.send(c)

    class Stream:
        def __init__(self, order, grad, temp, final, across=None):
            self.order, self.idx = order, index_of(order)
            self.grad, self.temp, self.final, self.across = grad, temp, final, across
            self.v, self.g = recvs.take(bits), recvs.take(nb)
            self.zv = recvs.take(Z) if across else None
            self.first, self.size, self.off = 0, chunks, 0

        def halve(self, k):
            if k < nb:
                self.size //= 2
                b = self.order[k]
                keep = self.first + bit_of(r, b) * self.size
                give = self.first + (1 - bit_of(r, b)) * self.size
            else:
                b, keep, give = k, self.first, self.first
            self.keep = keep
            self.at = len(pending)
            go(
                self.grad(give, self.size),
                self.temp(self.off, self.size),
                sends.take(1),
                self.v + k,
                (flip(r, b), z),
            )

        def add(self, k):
            got = self.temp(self.off, self.size)
            arrived(got, self.v + k)
            keep = self.grad(self.keep, self.size)
            if k >= nb:
                pending[self.at][0].wait_send()
                pending[self.at] = None
            deep = len(keep.shape) == 3
            for i in range(keep.shape[0] if deep else 1):
                a, b = (keep.at[i], got.at[i]) if deep else (keep, got)

                def step(j, carry):
                    a[blk(j, 16), :] = a[blk(j, 16), :] + b[blk(j, 16), :]
                    return carry

                lax.fori_loop(0, keep.shape[-2] // 16, step, 0)
            self.off += self.size
            self.first = self.keep

        def place(self):
            if self.across is None:
                self.put = local(self.grad(self.idx, 1), self.final(self.idx, 1))
                return
            src, dst = self.across
            for step in (2, 1, 3):
                t = lax.rem(z + step, Z)
                go(src(t, self.idx), dst(z, self.idx), sends.take(1), self.zv + z, (r, t))
            self.put = local(src(z, self.idx), dst(z, self.idx))

        def placed(self):
            if self.across is not None:
                for step in (1, 3, 2):
                    t = lax.rem(z + step, Z)
                    arrived(self.across[1](t, self.idx), self.zv + t)
            self.put.wait()

        def gather(self, k):
            size = 1 << k
            first = lax.div(self.idx, size) * size
            go(
                self.final(first, size),
                self.final(first, size),
                sends.take(1),
                self.g + k,
                (flip(r, self.order[nb - 1 - k]), z),
            )

        def gathered(self, k):
            size = 1 << k
            first = flip(lax.div(self.idx, size), 0) * size
            arrived(self.final(first, size), self.g + k)

    def wide_rows(ref, unit, lanes):
        return lambda first, n: ref.at[pl.ds(pl.multiple_of(first * unit, unit), n * unit), lanes]

    def deep_rows(ref, lanes):
        return lambda first, n: ref.at[:, pl.ds(pl.multiple_of(first * cr, cr), n * cr), lanes]

    def deep_block(ref, lanes):
        return lambda t, idx: ref.at[t, rows_at(idx * cr, cr), lanes]

    cd = FF // Z // chunks

    def pair(grad, temp, final, unit, width):
        made = []
        for order, lanes in ((order_a, pl.ds(0, width)), (order_b, pl.ds(width, width))):
            if unit:
                refs = [wide_rows(ref, unit, lanes) for ref in (grad, temp, final)]
                made.append(Stream(order, *refs))
            else:
                refs = [deep_rows(ref, lanes) for ref in (grad, temp, final)]
                both = (deep_block(grad, lanes), deep_block(final, lanes))
                made.append(Stream(order, *refs, both))
        return made

    class Group:
        def __init__(self, streams):
            self.streams, self.at = streams, 0

        def all(self, name, *args):
            for s in self.streams:
                getattr(s, name)(*args)

        def go_on(self, times=1):
            for _ in range(times):
                n = self.at
                if 0 < n <= bits:
                    self.all("add", n - 1)
                if n < bits:
                    self.all("halve", n)
                elif n == bits:
                    self.all("place")
                elif n == bits + 1:
                    self.all("placed")
                else:
                    self.all("gathered", n - bits - 2)
                if bits + 1 <= n < bits + 1 + nb:
                    self.all("gather", n - bits - 1)
                self.at += 1

    down = Group(pair(g_down, t_down, f_down, cd, 512) + pair(g_out, t_out, f_out, cr, 512))
    up = Group(pair(g_up, t_up, f_up, 0, 512))
    qkv = Group(pair(g_qkv, t_qkv, f_qkv, 0, 384))
    total_steps = bits + 2 + nb

    vec_steps = [(0, b) for b in range(bits)] + [(1, b) for b in range(2)]
    vec_v2 = recvs.take(len(vec_steps))
    vec_at = [0]

    def vec_on():
        n = vec_at[0]
        if n > len(vec_steps):
            return
        if n > 0:
            arrived(vrecv.at[n - 1], vec_v2 + n - 1)
            pending[vec_at[1]][0].wait_send()
            pending[vec_at[1]] = None
            vsum[...] = vsum[...] + vrecv[n - 1]
        if n < len(vec_steps):
            axis, b = vec_steps[n]
            dev = (flip(r, b), z) if axis == 0 else (r, flip(z, b))
            vec_at[1:] = [len(pending)]
            go(vsum, vrecv.at[n], sends.take(1), vec_v2 + n, dev)
        vec_at[0] += 1

    norm_rows(z)
    for j in range(1, Z):
        zz = lax.rem(z + j, Z)
        arrived(weight_region(0, zz, idx_a, 1), up_v + zz)
        for s in range(3):
            arrived(
                wqkv.at[rows_at(zz * LOC + idx_b * cr, cr), pl.ds(s * 256, 256)],
                qkv_v + zz * 3 + s,
            )
    for k in range(nb):
        weight_step(k)
        if k == nb - 1:
            gx.hand(c1, other)
            gx.hand(c2, end)
            gx.wait(c1)
            norm_rows(c1)
        weight_wait(k)
    project(z)
    project(c1)
    gx.hand(c3, end)
    gx.wait(c2)
    norm_rows(c2)
    project(c2)
    gx.wait(c3)
    gg.send()
    norm_rows(c3)
    project(c3)
    attend(c3)
    mix(c3)
    attend(c2)
    mix(c2)
    gg.hand(c1, other)
    gg.hand(c2, end)
    attend(c1)
    mix(c1)
    attend(z)
    mix(z)
    side(z)
    gg.wait(c1)
    side(c1)
    gg.hand(c3, end)
    s_out.pass_far(middle)
    gg.wait(c2)
    side(c2)
    s_out.pass_other(middle)
    gg.wait(c3)
    side(c3)
    g_out[...] = tn(ctx[...], og_all[...]).astype(BF)

    @pl.loop(0, Z)
    def _(c):
        g_down[blk(c, 256), :] = tn(hidden[:, blk(c, 256)], og_all[...]).astype(BF)

    down.go_on()
    s_out.pass_end(middle)
    back(3)
    down.go_on()
    back(2)
    down.go_on()

    @pl.loop(0, Z)
    def _(c):
        g_up[c] = tn(mlp_n[:, blk(c, 256)], dhid[...]).astype(BF)

    up.go_on()
    s_out.finish()
    outputs[...] = own_o[...].astype(BF)
    back(1)
    down.go_on()
    up.go_on()
    s_in.pass_far(z == 1)
    s_in.pass_other(z == 1)
    back(0)
    down.go_on()
    up.go_on()
    s_in.pass_end(z == 2)

    @pl.loop(0, Z)
    def _(c):
        g_qkv[c] = tn(attn_n[:, blk(c, 256)], dqkv[...]).astype(BF)

    qkv.go_on()
    s_in.pass_other(z == 2)

    def add_og(i, carry):
        return carry + og_all[rows_at(z * LOC + i * 16, 16), :].astype(F32)

    vsum[11:12, :] = jnp.sum(
        lax.fori_loop(0, LOC // 16, add_og, jnp.zeros((16, 1024), F32)), axis=0, keepdims=True
    )
    for k in range(4):
        vsum[k : k + 1, :] = jnp.sum(acc[k], axis=0, keepdims=True)
    vec_on()
    down.go_on()
    up.go_on()
    qkv.go_on()
    s_in.pass_far(z == 2)
    vec_on()
    down.go_on()
    up.go_on()
    qkv.go_on()
    vec_on()
    while qkv.at < total_steps:
        if down.at < total_steps:
            down.go_on()
        if up.at < total_steps:
            up.go_on()
        qkv.go_on()
        if qkv.at == bits + 2:
            s_in.pass_end(z == 1)
        vec_on()
    while vec_at[0] <= len(vec_steps):
        vec_on()
    vec_out[...] = vsum[...]
    s_in.finish()

    def finish(i, carry):
        rows = blk(i, 16)
        at = rows_at(z * LOC + i * 16, 16)
        rstd = rstd_s[at, :]
        xhat = (x_all[at, :].astype(F32) - mean_s[at, :]) * rstd
        g = own_i[rows, :]
        m1 = jnp.mean(g, axis=1, keepdims=True)
        m2 = jnp.mean(g * xhat, axis=1, keepdims=True)
        res = rstd * (g - m1 - xhat * m2)
        in_grad[rows, :] = (og_all[at, :].astype(F32) + res).astype(BF)
        return carry

    lax.fori_loop(0, LOC // 16, finish, 0, unroll=2)
    for copy, when in [p for p in pending if p is not None]:
        if when is None:
            copy.wait_send()
        else:
            pl.when(when)(copy.wait_send)


def tail(outs_in, in_in, f_qkv, f_up, f_out, f_down, vec, *results):
    z = lax.axis_index("shard")
    outs, ingrad, gga, gba, ggm, gbm, gqkv, gqkvb, gout, gup, gupb, gdown, goutb = results
    outs[...] = outs_in[...]
    ingrad[...] = in_in[...]
    for t in range(Z):
        gup[:, 1024 * t : 1024 * t + 1024] = f_up[t].astype(F32)
        for s in range(3):
            first = D * s + 256 * t
            gqkv[:, first : first + 256] = f_qkv[t, :, 256 * s : 256 * s + 256].astype(F32)
    gout[...] = f_out[...].astype(F32)
    gdown[...] = f_down[...].astype(F32)

    @pl.when(pl.program_id(0) == 0)
    def _():
        for k, ref in ((0, gga), (1, gba), (2, ggm), (3, gbm), (11, goutb)):
            ref[...] = vec[k : k + 1, blk(z, 256)]
        for i in range(3):
            g = 3 * z + i
            gqkvb[:, 256 * i : 256 * i + 256] = vec[pl.ds(4 + lax.div(g, Z), 1), blk(lax.rem(g, Z), 256)]
        gupb[...] = vec[pl.ds(7 + z, 1), :]


def shards(
    replicas,
    inputs,
    out_grad,
    segment_ids,
    ln_gain_attn,
    ln_bias_attn,
    ln_gain_mlp,
    ln_bias_mlp,
    qkv_weight,
    qkv_bias,
    out_weight,
    up_weight,
    up_bias,
    down_weight,
    output_bias,
):
    seg = segment_ids
    count0 = jnp.sum((seg == 0).astype(jnp.int32))
    count1 = jnp.sum((seg <= 1).astype(jnp.int32))
    start = jnp.where(seg == 0, 0, jnp.where(seg == 1, count0, count1))
    position = (lax.broadcasted_iota(jnp.int32, (1, TOK), 1) - start).astype(F32)
    half = ROT // 2
    freq = 1.0 / 10000.0 ** (jnp.arange(half, dtype=F32) * 2.0 / ROT)
    angles = freq[:, None] * position
    tab = jnp.concatenate(
        [jnp.cos(angles), jnp.sin(angles), jnp.broadcast_to(start.astype(F32), (8, TOK))], axis=0
    )
    vec = jnp.concatenate(
        [
            v.reshape(-1, 256)
            for v in (
                ln_gain_attn,
                ln_bias_attn,
                ln_gain_mlp,
                ln_bias_mlp,
                qkv_bias,
                output_bias,
                up_bias,
                jnp.zeros((4 * 256,), BF),
            )
        ],
        axis=0,
    )
    bits = int(math.log2(replicas))
    vm = pl.BlockSpec(memory_space=pltpu.VMEM)
    hbm = pl.BlockSpec(memory_space=pl.ANY)

    def v(*shape, dtype=BF):
        return pltpu.VMEM(shape, dtype)

    scratch = dict(
        x_all=v(TOK, D),
        og_all=v(TOK, D),
        vec_all=v(64, 256),
        tab=v(24, TOK, dtype=F32),
        tab_c=v(TOK, 128, dtype=F32),
        tab_a=v(TOK, 128, dtype=F32),
        tab_b=v(TOK, 128, dtype=F32),
        start=v(TOK, 1, dtype=F32),
        wqkv=v(D, 768),
        wup=v(D, 1024),
        wout=v(256, D),
        wdown=v(1024, D),
        attn_n=v(TOK, D),
        mlp_n=v(TOK, D),
        mean_s=v(TOK, 1, dtype=F32),
        rstd_s=v(TOK, 1, dtype=F32),
        q_s=v(TOK, 256),
        k_s=v(TOK, 256),
        v_s=v(TOK, 256),
        ctx=v(TOK, 256),
        lse=v(PAIRS, 2 * TOK, 1, dtype=F32),
        h32=v(LOC, 1024, dtype=F32),
        g32=v(LOC, 1024, dtype=F32),
        acc=v(4, 8, 1024, dtype=F32),
        hidden=v(TOK, 1024),
        dgelu=v(TOK, 1024),
        part_o=v(TOK, D),
        part_i=v(TOK, D),
        own_o=v(LOC, D, dtype=F32),
        own_i=v(LOC, D, dtype=F32),
        land_o=v(5 * LOC, D),
        land_i=v(5 * LOC, D),
        gctx=v(TOK, 256),
        dq=v(TOK, 256, dtype=F32),
        dk=v(TOK, 256, dtype=F32),
        dv=v(TOK, 256, dtype=F32),
        dqkv=v(TOK, 768),
        g_qkv=v(Z, 256, 768),
        g_up=v(Z, 256, 1024),
        g_out=v(256, D),
        g_down=v(1024, D),
        t_qkv=v(Z, 256, 768),
        t_up=v(Z, 256, 1024),
        t_out=v(256, D),
        t_down=v(1024, D),
        vsum=v(16, 1024, dtype=F32),
        vrecv=v(bits + 2, 16, 1024, dtype=F32),
        ssem=pltpu.SemaphoreType.DMA((NSEM,)),
        rsem=pltpu.SemaphoreType.DMA((NSEM,)),
        lsem=pltpu.SemaphoreType.DMA((32,)),
    )
    names = list(scratch)

    def body(*refs):
        layer(replicas, *refs[:15], **dict(zip(names, refs[15:])))

    res = pl.pallas_call(
        body,
        out_shape=[
            jax.ShapeDtypeStruct((LOC, D), BF),
            jax.ShapeDtypeStruct((LOC, D), BF),
            jax.ShapeDtypeStruct((Z, 256, 768), BF),
            jax.ShapeDtypeStruct((Z, 256, 1024), BF),
            jax.ShapeDtypeStruct((256, D), BF),
            jax.ShapeDtypeStruct((1024, D), BF),
            jax.ShapeDtypeStruct((16, 1024), F32),
        ],
        in_specs=[hbm] * 8,
        out_specs=[vm, vm, hbm, hbm, hbm, hbm, vm],
        scratch_shapes=list(scratch.values()),
        compiler_params=pltpu.CompilerParams(
            collective_id=0,
            has_side_effects=True,
            vmem_limit_bytes=61 * 2**20,
        ),
    )(
        inputs.reshape(LOC, D),
        out_grad.reshape(LOC, D),
        qkv_weight,
        up_weight,
        out_weight,
        down_weight,
        vec,
        tab,
    )
    steps = 8
    n = LOC // steps
    row = pl.BlockSpec((n, D), lambda i: (i, 0))
    tall = pl.BlockSpec((1024 // steps, D), lambda i: (i, 0))

    def fixed(w):
        return pl.BlockSpec((1, w), lambda i: (0, 0))

    small, wide = [fixed(256)], [fixed(768)]
    final = pl.pallas_call(
        tail,
        grid=(steps,),
        in_specs=[
            row,
            row,
            pl.BlockSpec((Z, n, 768), lambda i: (0, i, 0)),
            pl.BlockSpec((Z, n, 1024), lambda i: (0, i, 0)),
            row,
            tall,
            pl.BlockSpec((16, 1024), lambda i: (0, 0)),
        ],
        out_specs=[row, row]
        + small * 4
        + [pl.BlockSpec((n, 3 * D), lambda i: (i, 0))]
        + wide
        + [row, pl.BlockSpec((n, FF), lambda i: (i, 0)), fixed(1024), tall]
        + small,
        out_shape=[jax.ShapeDtypeStruct((LOC, D), BF)] * 2
        + [jax.ShapeDtypeStruct((1, 256), F32)] * 4
        + [
            jax.ShapeDtypeStruct((256, 3 * D), F32),
            jax.ShapeDtypeStruct((1, 768), F32),
            jax.ShapeDtypeStruct((256, D), F32),
            jax.ShapeDtypeStruct((256, FF), F32),
            jax.ShapeDtypeStruct((1, 1024), F32),
            jax.ShapeDtypeStruct((1024, D), F32),
            jax.ShapeDtypeStruct((1, 256), F32),
        ],
    )(*res)
    shapes = [(1, LOC, D)] * 2 + [(256,)] * 4 + [None, (768,), None, None, (1024,), None, (256,)]
    return tuple(a if s is None else a.reshape(s) for a, s in zip(final, shapes))


def solution(mesh):
    seq = P("replica", "shard", None)
    row = P("shard", None)
    one = P("shard")
    return jax.shard_map(
        partial(shards, mesh.shape["replica"]),
        mesh=mesh,
        in_specs=(seq, seq, P("replica", None), one, one, one, one, row, one, row, row, one, row, one),
        out_specs=(seq, seq, one, one, one, one, row, one, row, row, one, row, one),
        check_vma=False,
    )
```

time: 269 us -> 208 us (0.77); the launches traced: 269 us -> 205 us
  Pallas kernels: 238 us -> 193 us
  other arithmetic: 15.4 us -> 5.47 us
  local copies, waits for them, and re-layouts: 14.5 us -> 5.92 us
    pallas_call x1 -> x2, Pallas kernels: 238 us -> 193 us  [the longest x1 183 us: shards(): pl.pallas_call(body, out_shape=[jax.ShapeDtypeStruct((LOC, D), BF), jax.S...]
    convert_element_type x5 -> x2, other arithmetic: 9.84 us -> 1.99 us  [the longest x1 1.99 us: shards(): (lax.broadcasted_iota(jnp.int32, (1, TOK), 1) - start).astype(F32)]
    dynamic_slice x7 -> x0, local copies, waits for them, and re-layouts: 4.09 us -> none  [cut(): return lax.dynamic_slice_in_dim(first, z * n, n, 0)]
    reshape x2 -> x8, local copies, waits for them, and re-layouts: 0.62 us -> 4.68 us  [shards(): v.reshape(-1, 256)]
    unnamed x36 -> x0, local copies, waits for them, and re-layouts: 3.75 us -> none
    select_n x2 -> x0, other arithmetic: 3.28 us -> none  [shards(): start = jnp.where(seg == 0, 0, jnp.where(seg == 1, count0, count1))]
    another operation x6 -> x0, local copies, waits for them, and re-layouts: 3.12 us -> none  [the longest x2 1.04 us: shards(): tab_a = jnp.tile(jnp.concatenate([-sine, none, pad0], axis=1), (1, 2))]
where the time goes in v2:
time: 208 us; the launch traced here: 205 us
  Pallas kernels  193 us (93%)
  local copies, waits for them, and re-layouts  5.92 us (3%)
  other arithmetic  5.47 us (3%)
    pallas_call x1, Pallas kernels, shards(): pl.pallas_call(body, out_shape=[jax.ShapeDtypeStruct((LOC, D), BF), jax.S...  183 us
    pallas_call x1, Pallas kernels, shards(): pl.pallas_call(tail, grid=(steps,), in_specs=[row, row, pl.BlockSpec((Z,...  9.52 us
    reshape x8, local copies, waits for them, and re-layouts, shards(): v.reshape(-1, 256)  4.68 us

profile of v2, /device:TPU:0, one launch (start us, length us, event | category | flops | bytes accessed | tf_op | source)
XLA Modules:
  0.0 204.9 jit_solution(8784556998612266773)
XLA Ops:
  0.7 0.7 reshape.91
  1.3 0.7 reshape.92
  2.0 0.7 reshape.93
  2.6 0.7 reshape.94
  3.3 0.7 reshape.96
  4.0 1.3 fusion
  5.3 0.7 reshape.95
  6.0 0.7 reshape.97
  6.7 1.2 concatenate.6.refs_6_
  7.9 2.0 subtract_convert_fusion
  9.9 0.2 multiply_cosine_fusion
  10.1 0.7 pad_maximum_fusion.refs_7_
  10.8 183.3 %shard_map.237 = (bf16[256,1024]{1,0:T(8,128)(2,1)}, bf16[256,1024]{1,0:T(8,128)(2,1)}, bf16[4,256,768]{2,1,0:T(8,128)(2,1)}, bf16[4,256,1024]{2,1,0:T(8,128)(2,...) custom-call(bf16[256,1024]{1,0:T(8,128)(2,1)} %bitcast.12, ...), custom_call_target="tpu_custom_call" | custom-call | tf_op jit(solution)/shard_map/pallas_call | solution.py:1000
  194.1 9.5 %shard_map.238 = (bf16[256,1024]{1,0:T(8,128)(2,1)}, bf16[256,1024]{1,0:T(8,128)(2,1)}, f32[1,256]{1,0:T(1,128)}, f32[1,256]{1,0:T(1,128)}, f32[1,256]{1,0:T(1,1...) custom-call(bf16[256,1024]{1,0:T(8,128)(2,1)} %get-tuple-element.33., ...), custom_call_target="tpu_custom_call" | custom-call | tf_op jit(solution)/shard_map/pallas_call | solution.py:1038
  203.6 1.3 reduce
  (4 shorter events, 0.0 us)

commit v3 on v2

--- a/solution.py
+++ b/solution.py
@@ -3,6 +3,7 @@
 
 import jax
 import jax.numpy as jnp
+import numpy as np
 from jax import lax
 from jax.experimental import pallas as pl
 from jax.experimental.pallas import tpu as pltpu
@@ -70,19 +71,30 @@
     up_w,
     out_w,
     down_w,
-    vec_in,
-    tab_in,
+    gain_a_in,
+    bias_a_in,
+    gain_m_in,
+    bias_m_in,
+    bias_o_in,
+    qkv_b_in,
+    up_b_in,
+    seg_in,
     outputs,
     in_grad,
     f_qkv,
     f_up,
-    f_out,
-    f_down,
+    f_od,
     vec_out,
     x_all,
     og_all,
-    vec_all,
-    tab,
+    gain_a_all,
+    bias_a_all,
+    gain_m_all,
+    bias_m_all,
+    bias_o_all,
+    qkv_b_all,
+    up_b,
+    seg,
     tab_c,
     tab_a,
     tab_b,
@@ -118,12 +130,10 @@
     dqkv,
     g_qkv,
     g_up,
-    g_out,
-    g_down,
+    g_od,
     t_qkv,
     t_up,
-    t_out,
-    t_down,
+    t_od,
     vsum,
     vrecv,
     ssem,
@@ -182,8 +192,20 @@
     def rows_at(first, n):
         return pl.ds(pl.multiple_of(first, n), n)
 
-    vec_own = local(vec_in, vec_all.at[blk(z, 16)])
-    tab_own = local(tab_in, tab)
+    small = [
+        (gain_a_in, gain_a_all),
+        (bias_a_in, bias_a_all),
+        (gain_m_in, gain_m_all),
+        (bias_m_in, bias_m_all),
+        (bias_o_in, bias_o_all),
+        (qkv_b_in, qkv_b_all),
+    ]
+
+    def share(ref, src, c):
+        return ref.at[blk(c, src.shape[0])]
+
+    vec_own = [local(src, share(dst, src, z)) for src, dst in small] + [local(up_b_in, up_b)]
+    seg_own = local(seg_in, seg)
     x_own = local(x_in, x_all.at[own_rows])
 
     barrier = pltpu.get_barrier_semaphore()
@@ -204,10 +226,11 @@
     idx_a, idx_b = index_of(order_a), index_of(order_b)
     cr = LOC // chunks
 
-    up_v, qkv_v, vec_v = recvs.take(Z), recvs.take(3 * Z), recvs.take(Z)
+    up_v, qkv_v, vec_v = recvs.take(Z), recvs.take(3 * Z), recvs.take(6 * Z)
     for step in (1, 3, 2):
         t = lax.rem(z + step, Z)
-        go(vec_in, vec_all.at[blk(z, 16)], sends.take(1), vec_v + z, (r, t))
+        for i, (src, dst) in enumerate(small):
+            go(src, share(dst, src, z), sends.take(1), vec_v + i * Z + z, (r, t))
     for step in (1, 3, 2):
         t = lax.rem(z + step, Z)
         go(
@@ -303,20 +326,25 @@
                 first = flip(lax.div(idx, size), 0) * size
                 arrived(weight_region(kind, zz, first, size), ag_v + ((j - 1) * 2 + kind) * nb + k)
 
-    tab_own.wait()
-    vec_own.wait()
-    x_own.wait()
-    own_up.wait()
-    og_own.wait()
-    for copy in own_qkv + w_own:
-        copy.wait()
+    seg_own.wait()
     lane = lax.broadcasted_iota(jnp.int32, (QB, 128), 1)
     turned = lax.rem(lane, HEAD) < ROT
-
-    @pl.loop(0, TOK // 128)
-    def _(i):
-        at = blk(i, 128)
-        cosine, sine, first = tab[0:8, at], tab[8:16, at], tab[16:24, at]
+    ids = seg[...]
+    count0 = jnp.sum((ids == 0).astype(F32), axis=1, keepdims=True)
+    count1 = jnp.sum((ids <= 1).astype(F32), axis=1, keepdims=True)
+    begin = jnp.where(ids == 0, 0.0, jnp.where(ids == 1, count0, count1))
+    begin8 = jnp.broadcast_to(begin, (8, TOK))
+    position = lax.broadcasted_iota(jnp.int32, (8, TOK), 1).astype(F32) - begin8
+    turn = lax.broadcasted_iota(jnp.int32, (8, TOK), 0)
+    freq = jnp.zeros((8, TOK), F32)
+    for i in range(ROT // 2):
+        rate = np.float32(1.0) / np.float32(10000.0) ** np.float32(i * 2.0 / ROT)
+        freq = jnp.where(turn == i, float(rate), freq)
+    angles = position * freq
+    cosines, sines = jnp.cos(angles), jnp.sin(angles)
+    for i in range(TOK // 128):
+        at = slice(128 * i, 128 * i + 128)
+        cosine, sine, first = cosines[:, at], sines[:, at], begin8[:, at]
         none = jnp.zeros_like(cosine)
         half = [cosine, cosine, -sine, none, none, sine, first, none]
         wide = jnp.concatenate(half + half, axis=0).T
@@ -325,24 +353,20 @@
         tab_b[at, :] = jnp.where(turned, pltpu.roll(wide, 96, 1), 0.0)
         start[at, :] = wide[:, 48:49]
 
+    for copy in vec_own:
+        copy.wait()
+    x_own.wait()
     for j in range(1, Z):
         zz = lax.rem(z + j, Z)
-        arrived(vec_all.at[blk(zz, 16)], vec_v + zz)
-
-    def vector(row):
-        return jnp.concatenate(
-            [vec_all[16 * c : 16 * c + 16, :][row : row + 1, :] for c in range(Z)], axis=1
-        ).astype(F32)
-
-    def vector256(i):
-        block = vec_all[blk(lax.div(i, 3), 16), :].astype(F32)
-        rows = lax.broadcasted_iota(jnp.int32, (16, 256), 0)
-        return jnp.sum(jnp.where(rows == 4 + lax.rem(i, 3), block, 0.0), axis=0, keepdims=True)
-
-    gain_a, bias_a, gain_m, bias_m, bias_o = [vector(i) for i in (0, 1, 2, 3, 7)]
-    qkv_b = [vector256(s * Z + z) for s in range(3)]
-    mine = vec_all[blk(z, 16), :]
-    up_shift = jnp.concatenate([mine[8 + i : 9 + i, :] for i in range(4)], axis=1).astype(F32)
+        for i, (src, dst) in enumerate(small):
+            arrived(share(dst, src, zz), vec_v + i * Z + zz)
+
+    def flat(piece):
+        return piece.astype(F32).reshape(1, piece.shape[0])
+
+    gain_a, bias_a, gain_m, bias_m, bias_o = [flat(dst[...]) for _, dst in small[:5]]
+    qkv_b = [flat(qkv_b_all[blk(s * Z + z, 256)]) for s in range(3)]
+    up_shift = flat(up_b[...])
 
     def norm_rows(c):
         def norm(i, carry):
@@ -527,7 +551,7 @@
 
     dhid = dgelu
 
-    def back(c):
+    def attend_back(c):
         @pl.loop(0, LOC // QB)
         def _(j):
             i = c * (LOC // QB) + j
@@ -547,15 +571,21 @@
                 dk[keys, lanes] += tn(ds, q2)
                 dv[keys, lanes] += tn(prob.astype(BF), g2)
 
+    def turn_back():
+        @pl.loop(0, Z)
+        def _(c):
+            rows = blk(c, LOC)
+            for p in range(PAIRS):
+                lanes = slice(128 * p, 128 * p + 128)
+                dqkv[rows, lanes] = rotate(dq[rows, lanes], rows, -1.0).astype(BF)
+                dqkv[rows, 256 + 128 * p : 384 + 128 * p] = rotate(dk[rows, lanes], rows, -1.0).astype(BF)
+            dqkv[rows, 512:] = dv[rows, :].astype(BF)
+            sums = jnp.sum(dqkv[rows, :].astype(F32), axis=0, keepdims=True)
+            for s in range(3):
+                vsum[4 + s : 5 + s, blk(z, 256)] += sums[:, 256 * s : 256 * s + 256]
+
+    def inward(c):
         rows = blk(c, LOC)
-        for p in range(PAIRS):
-            lanes = slice(128 * p, 128 * p + 128)
-            dqkv[rows, lanes] = rotate(dq[rows, lanes], rows, -1.0).astype(BF)
-            dqkv[rows, 256 + 128 * p : 384 + 128 * p] = rotate(dk[rows, lanes], rows, -1.0).astype(BF)
-        dqkv[rows, 512:] = dv[rows, :].astype(BF)
-        sums = jnp.sum(dqkv[rows, :].astype(F32), axis=0, keepdims=True)
-        for s in range(3):
-            vsum[4 + s : 5 + s, blk(z, 256)] += sums[:, 256 * s : 256 * s + 256]
         g32[...] = nt(dqkv[rows, :], wqkv[...])
         h32[...] = nt(dhid[rows, :], wup[...])
 
@@ -564,20 +594,45 @@
             here = blk(i, 16)
             xhat = (x_all[at, :].astype(F32) - mean_s[at, :]) * rstd_s[at, :]
             ga, gm = g32[here, :], h32[here, :]
-            for k, v in enumerate((ga * xhat, ga, gm * xhat, gm)):
+            for k, v in enumerate((ga * xhat, gm * xhat)):
                 acc[k] += v[:8] + v[8:]
             g = ga * gain_a + gm * gain_m
-            g32[here, :] = g
-            part_i[at, :] = g.astype(BF)
+            if c is z:
+                own_i[here, :] = g
+            else:
+                part_i[at, :] = g.astype(BF)
             return carry
 
         lax.fori_loop(0, LOC // 16, step, 0)
 
-        @pl.when(z == c)
-        def _():
-            own_i[...] = g32[...]
-
-        s_in.send(c)
+    def through(sums, weight):
+        parts, rest = [], sums
+        for _ in range(3):
+            part = rest.astype(BF).astype(F32)
+            parts.append(part)
+            rest = rest - part
+        parts.append(jnp.zeros((13, sums.shape[1]), F32))
+        return jnp.sum(nt(jnp.concatenate(parts, axis=0).astype(BF), weight[...]), axis=0, keepdims=True)
+
+    cd = FF // Z // chunks
+
+    def weights_down():
+        g_od[:, cd:, :] = tn(ctx[...], og_all[...]).reshape(chunks, cr, D).astype(BF)
+
+        @pl.loop(0, Z)
+        def _(i):
+            got = tn(hidden[:, blk(i, 256)], og_all[...])
+            g_od[blk(i, 256 // cd), :cd, :] = got.reshape(256 // cd, cd, D).astype(BF)
+
+    def weights_up():
+        @pl.loop(0, Z)
+        def _(i):
+            g_up[i] = tn(mlp_n[:, blk(i, 256)], dhid[...]).astype(BF)
+
+    def weights_qkv():
+        @pl.loop(0, Z)
+        def _(c):
+            g_qkv[c] = tn(attn_n[:, blk(c, 256)], dqkv[...]).astype(BF)
 
     class Stream:
         def __init__(self, order, grad, temp, final, across=None):
@@ -612,15 +667,14 @@
             if k >= nb:
                 pending[self.at][0].wait_send()
                 pending[self.at] = None
-            deep = len(keep.shape) == 3
-            for i in range(keep.shape[0] if deep else 1):
-                a, b = (keep.at[i], got.at[i]) if deep else (keep, got)
-
-                def step(j, carry):
-                    a[blk(j, 16), :] = a[blk(j, 16), :] + b[blk(j, 16), :]
-                    return carry
-
-                lax.fori_loop(0, keep.shape[-2] // 16, step, 0)
+            n = keep.shape[1] // 16
+
+            def step(j, carry):
+                i, at = lax.div(j, n), blk(lax.rem(j, n), 16)
+                keep[i, at, :] = keep[i, at, :] + got[i, at, :]
+                return carry
+
+            lax.fori_loop(0, keep.shape[0] * n, step, 0, unroll=4)
             self.off += self.size
             self.first = self.keep
 
@@ -657,8 +711,8 @@
             first = flip(lax.div(self.idx, size), 0) * size
             arrived(self.final(first, size), self.g + k)
 
-    def wide_rows(ref, unit, lanes):
-        return lambda first, n: ref.at[pl.ds(pl.multiple_of(first * unit, unit), n * unit), lanes]
+    def chunk_rows(ref, lanes):
+        return lambda first, n: ref.at[pl.ds(first, n), :, lanes]
 
     def deep_rows(ref, lanes):
         return lambda first, n: ref.at[:, pl.ds(pl.multiple_of(first * cr, cr), n * cr), lanes]
@@ -666,18 +720,15 @@
     def deep_block(ref, lanes):
         return lambda t, idx: ref.at[t, rows_at(idx * cr, cr), lanes]
 
-    cd = FF // Z // chunks
-
-    def pair(grad, temp, final, unit, width):
+    def pair(grad, temp, final, width, across):
         made = []
         for order, lanes in ((order_a, pl.ds(0, width)), (order_b, pl.ds(width, width))):
-            if unit:
-                refs = [wide_rows(ref, unit, lanes) for ref in (grad, temp, final)]
-                made.append(Stream(order, *refs))
-            else:
+            if across:
                 refs = [deep_rows(ref, lanes) for ref in (grad, temp, final)]
                 both = (deep_block(grad, lanes), deep_block(final, lanes))
                 made.append(Stream(order, *refs, both))
+            else:
+                made.append(Stream(order, *[chunk_rows(ref, lanes) for ref in (grad, temp, final)]))
         return made
 
     class Group:
@@ -705,9 +756,9 @@
                     self.all("gather", n - bits - 1)
                 self.at += 1
 
-    down = Group(pair(g_down, t_down, f_down, cd, 512) + pair(g_out, t_out, f_out, cr, 512))
-    up = Group(pair(g_up, t_up, f_up, 0, 512))
-    qkv = Group(pair(g_qkv, t_qkv, f_qkv, 0, 384))
+    down = Group(pair(g_od, t_od, f_od, 512, False))
+    up = Group(pair(g_up, t_up, f_up, 512, True))
+    qkv = Group(pair(g_qkv, t_qkv, f_qkv, 384, True))
     total_steps = bits + 2 + nb
 
     vec_steps = [(0, b) for b in range(bits)] + [(1, b) for b in range(2)]
@@ -741,15 +792,19 @@
             )
     for k in range(nb):
         weight_step(k)
-        if k == nb - 1:
+        if k == 1:
             gx.hand(c1, other)
             gx.hand(c2, end)
+        if k == nb - 1:
             gx.wait(c1)
             norm_rows(c1)
         weight_wait(k)
+    own_up.wait()
+    for copy in own_qkv:
+        copy.wait()
+    gx.hand(c3, end)
     project(z)
     project(c1)
-    gx.hand(c3, end)
     gx.wait(c2)
     norm_rows(c2)
     project(c2)
@@ -757,6 +812,8 @@
     gg.send()
     norm_rows(c3)
     project(c3)
+    for copy in w_own:
+        copy.wait()
     attend(c3)
     mix(c3)
     attend(c2)
@@ -767,52 +824,44 @@
     mix(c1)
     attend(z)
     mix(z)
+    og_own.wait()
     side(z)
     gg.wait(c1)
     side(c1)
     gg.hand(c3, end)
+    attend_back(z)
+    attend_back(c1)
     s_out.pass_far(middle)
     gg.wait(c2)
     side(c2)
+    attend_back(c2)
     s_out.pass_other(middle)
     gg.wait(c3)
+    weights_down()
+    down.go_on()
     side(c3)
-    g_out[...] = tn(ctx[...], og_all[...]).astype(BF)
-
-    @pl.loop(0, Z)
-    def _(c):
-        g_down[blk(c, 256), :] = tn(hidden[:, blk(c, 256)], og_all[...]).astype(BF)
-
-    down.go_on()
-    s_out.pass_end(middle)
-    back(3)
-    down.go_on()
-    back(2)
-    down.go_on()
-
-    @pl.loop(0, Z)
-    def _(c):
-        g_up[c] = tn(mlp_n[:, blk(c, 256)], dhid[...]).astype(BF)
-
-    up.go_on()
-    s_out.finish()
-    outputs[...] = own_o[...].astype(BF)
-    back(1)
+    weights_up()
     down.go_on()
     up.go_on()
-    s_in.pass_far(z == 1)
-    s_in.pass_other(z == 1)
-    back(0)
+    attend_back(c3)
+    up.go_on()
+    s_out.pass_end(middle)
+    turn_back()
+    weights_qkv()
+    qkv.go_on()
     down.go_on()
+    inward(c3)
+    s_in.send(c3)
+    qkv.go_on()
+    inward(c2)
+    down.go_on(2)
     up.go_on()
-    s_in.pass_end(z == 2)
-
-    @pl.loop(0, Z)
-    def _(c):
-        g_qkv[c] = tn(attn_n[:, blk(c, 256)], dqkv[...]).astype(BF)
-
+    inward(c1)
+    s_in.send(c2)
+    inward(z)
+    up.go_on()
+    down.go_on()
     qkv.go_on()
-    s_in.pass_other(z == 2)
 
     def add_og(i, carry):
         return carry + og_all[rows_at(z * LOC + i * 16, 16), :].astype(F32)
@@ -820,30 +869,35 @@
     vsum[11:12, :] = jnp.sum(
         lax.fori_loop(0, LOC // 16, add_og, jnp.zeros((16, 1024), F32)), axis=0, keepdims=True
     )
-    for k in range(4):
-        vsum[k : k + 1, :] = jnp.sum(acc[k], axis=0, keepdims=True)
+    sums = jnp.concatenate([vsum[4 + s : 5 + s, blk(z, 256)] for s in range(3)], axis=1)
+    vsum[0:1, :] = jnp.sum(acc[0], axis=0, keepdims=True)
+    vsum[1:2, :] = through(sums, wqkv)
+    vsum[2:3, :] = jnp.sum(acc[1], axis=0, keepdims=True)
+    vsum[3:4, :] = through(vsum[pl.ds(7 + z, 1), :], wup)
     vec_on()
+    s_in.pass_far(middle)
+    s_out.finish()
+    part_o[own_rows, :] = own_o[...].astype(BF)
+    copies = [local(part_o.at[own_rows], outputs)]
+    qkv.go_on()
+    up.go_on()
+    vec_on()
+    s_in.send(c1)
     down.go_on()
-    up.go_on()
-    qkv.go_on()
-    s_in.pass_far(z == 2)
+    s_in.pass_other(middle)
     vec_on()
-    down.go_on()
     up.go_on()
     qkv.go_on()
     vec_on()
-    while qkv.at < total_steps:
+    s_in.pass_end(middle)
+    while qkv.at < total_steps - 1:
+        qkv.go_on()
+        vec_on()
+        if up.at < total_steps:
+            up.go_on()
         if down.at < total_steps:
             down.go_on()
-        if up.at < total_steps:
-            up.go_on()
-        qkv.go_on()
-        if qkv.at == bits + 2:
-            s_in.pass_end(z == 1)
-        vec_on()
-    while vec_at[0] <= len(vec_steps):
-        vec_on()
-    vec_out[...] = vsum[...]
+    vec_on()
     s_in.finish()
 
     def finish(i, carry):
@@ -855,10 +909,19 @@
         m1 = jnp.mean(g, axis=1, keepdims=True)
         m2 = jnp.mean(g * xhat, axis=1, keepdims=True)
         res = rstd * (g - m1 - xhat * m2)
-        in_grad[rows, :] = (og_all[at, :].astype(F32) + res).astype(BF)
+        part_i[at, :] = (og_all[at, :].astype(F32) + res).astype(BF)
         return carry
 
     lax.fori_loop(0, LOC // 16, finish, 0, unroll=2)
+    copies.append(local(part_i.at[own_rows], in_grad))
+    while vec_at[0] <= len(vec_steps):
+        vec_on()
+    vec_out[...] = vsum[...]
+    for group in (qkv, up, down):
+        while group.at < total_steps:
+            group.go_on()
+    for copy in copies:
+        copy.wait()
     for copy, when in [p for p in pending if p is not None]:
         if when is None:
             copy.wait_send()
@@ -866,7 +929,7 @@
             pl.when(when)(copy.wait_send)
 
 
-def tail(outs_in, in_in, f_qkv, f_up, f_out, f_down, vec, *results):
+def tail(outs_in, in_in, f_qkv, f_up, f_od, vec, *results):
     z = lax.axis_index("shard")
     outs, ingrad, gga, gba, ggm, gbm, gqkv, gqkvb, gout, gup, gupb, gdown, goutb = results
     outs[...] = outs_in[...]
@@ -876,17 +939,20 @@
         for s in range(3):
             first = D * s + 256 * t
             gqkv[:, first : first + 256] = f_qkv[t, :, 256 * s : 256 * s + 256].astype(F32)
-    gout[...] = f_out[...].astype(F32)
-    gdown[...] = f_down[...].astype(F32)
+    n, m = gdown.shape[0] // f_od.shape[0], gout.shape[0] // f_od.shape[0]
+    for i in range(f_od.shape[0]):
+        gdown[n * i : n * i + n, :] = f_od[i, :n].astype(F32)
+        gout[m * i : m * i + m, :] = f_od[i, n:].astype(F32)
 
     @pl.when(pl.program_id(0) == 0)
     def _():
         for k, ref in ((0, gga), (1, gba), (2, ggm), (3, gbm), (11, goutb)):
-            ref[...] = vec[k : k + 1, blk(z, 256)]
+            ref[...] = vec[k : k + 1, blk(z, 256)].reshape(256)
         for i in range(3):
             g = 3 * z + i
-            gqkvb[:, 256 * i : 256 * i + 256] = vec[pl.ds(4 + lax.div(g, Z), 1), blk(lax.rem(g, Z), 256)]
-        gupb[...] = vec[pl.ds(7 + z, 1), :]
+            piece = vec[pl.ds(4 + lax.div(g, Z), 1), blk(lax.rem(g, Z), 256)]
+            gqkvb[256 * i : 256 * i + 256] = piece.reshape(256)
+        gupb[...] = vec[pl.ds(7 + z, 1), :].reshape(1024)
 
 
 def shards(
@@ -906,34 +972,8 @@
     down_weight,
     output_bias,
 ):
-    seg = segment_ids
-    count0 = jnp.sum((seg == 0).astype(jnp.int32))
-    count1 = jnp.sum((seg <= 1).astype(jnp.int32))
-    start = jnp.where(seg == 0, 0, jnp.where(seg == 1, count0, count1))
-    position = (lax.broadcasted_iota(jnp.int32, (1, TOK), 1) - start).astype(F32)
-    half = ROT // 2
-    freq = 1.0 / 10000.0 ** (jnp.arange(half, dtype=F32) * 2.0 / ROT)
-    angles = freq[:, None] * position
-    tab = jnp.concatenate(
-        [jnp.cos(angles), jnp.sin(angles), jnp.broadcast_to(start.astype(F32), (8, TOK))], axis=0
-    )
-    vec = jnp.concatenate(
-        [
-            v.reshape(-1, 256)
-            for v in (
-                ln_gain_attn,
-                ln_bias_attn,
-                ln_gain_mlp,
-                ln_bias_mlp,
-                qkv_bias,
-                output_bias,
-                up_bias,
-                jnp.zeros((4 * 256,), BF),
-            )
-        ],
-        axis=0,
-    )
     bits = int(math.log2(replicas))
+    chunks = 1 << min(bits, 4)
     vm = pl.BlockSpec(memory_space=pltpu.VMEM)
     hbm = pl.BlockSpec(memory_space=pl.ANY)
 
@@ -943,8 +983,14 @@
     scratch = dict(
         x_all=v(TOK, D),
         og_all=v(TOK, D),
-        vec_all=v(64, 256),
-        tab=v(24, TOK, dtype=F32),
+        gain_a_all=v(D),
+        bias_a_all=v(D),
+        gain_m_all=v(D),
+        bias_m_all=v(D),
+        bias_o_all=v(D),
+        qkv_b_all=v(3 * D),
+        up_b=v(1024),
+        seg=pltpu.VMEM((1, TOK), jnp.int32),
         tab_c=v(TOK, 128, dtype=F32),
         tab_a=v(TOK, 128, dtype=F32),
         tab_b=v(TOK, 128, dtype=F32),
@@ -964,7 +1010,7 @@
         lse=v(PAIRS, 2 * TOK, 1, dtype=F32),
         h32=v(LOC, 1024, dtype=F32),
         g32=v(LOC, 1024, dtype=F32),
-        acc=v(4, 8, 1024, dtype=F32),
+        acc=v(2, 8, 1024, dtype=F32),
         hidden=v(TOK, 1024),
         dgelu=v(TOK, 1024),
         part_o=v(TOK, D),
@@ -980,12 +1026,10 @@
         dqkv=v(TOK, 768),
         g_qkv=v(Z, 256, 768),
         g_up=v(Z, 256, 1024),
-        g_out=v(256, D),
-        g_down=v(1024, D),
+        g_od=v(chunks, 1280 // chunks, D),
         t_qkv=v(Z, 256, 768),
         t_up=v(Z, 256, 1024),
-        t_out=v(256, D),
-        t_down=v(1024, D),
+        t_od=v(chunks, 1280 // chunks, D),
         vsum=v(16, 1024, dtype=F32),
         vrecv=v(bits + 2, 16, 1024, dtype=F32),
         ssem=pltpu.SemaphoreType.DMA((NSEM,)),
@@ -995,7 +1039,7 @@
     names = list(scratch)
 
     def body(*refs):
-        layer(replicas, *refs[:15], **dict(zip(names, refs[15:])))
+        layer(replicas, *refs[:20], **dict(zip(names, refs[20:])))
 
     res = pl.pallas_call(
         body,
@@ -1004,12 +1048,11 @@
             jax.ShapeDtypeStruct((LOC, D), BF),
             jax.ShapeDtypeStruct((Z, 256, 768), BF),
             jax.ShapeDtypeStruct((Z, 256, 1024), BF),
-            jax.ShapeDtypeStruct((256, D), BF),
-            jax.ShapeDtypeStruct((1024, D), BF),
+            jax.ShapeDtypeStruct((chunks, 1280 // chunks, D), BF),
             jax.ShapeDtypeStruct((16, 1024), F32),
         ],
-        in_specs=[hbm] * 8,
-        out_specs=[vm, vm, hbm, hbm, hbm, hbm, vm],
+        in_specs=[hbm] * 14,
+        out_specs=[hbm, hbm, hbm, hbm, hbm, vm],
         scratch_shapes=list(scratch.values()),
         compiler_params=pltpu.CompilerParams(
             collective_id=0,
@@ -1023,16 +1066,22 @@
         up_weight,
         out_weight,
         down_weight,
-        vec,
-        tab,
+        ln_gain_attn,
+        ln_bias_attn,
+        ln_gain_mlp,
+        ln_bias_mlp,
+        output_bias,
+        qkv_bias,
+        up_bias,
+        segment_ids,
     )
-    steps = 8
+    steps = chunks // 2
     n = LOC // steps
     row = pl.BlockSpec((n, D), lambda i: (i, 0))
     tall = pl.BlockSpec((1024 // steps, D), lambda i: (i, 0))
 
     def fixed(w):
-        return pl.BlockSpec((1, w), lambda i: (0, 0))
+        return pl.BlockSpec((w,), lambda i: (0,))
 
     small, wide = [fixed(256)], [fixed(768)]
     final = pl.pallas_call(
@@ -1043,8 +1092,7 @@
             row,
             pl.BlockSpec((Z, n, 768), lambda i: (0, i, 0)),
             pl.BlockSpec((Z, n, 1024), lambda i: (0, i, 0)),
-            row,
-            tall,
+            pl.BlockSpec((2, 1280 // chunks, D), lambda i: (i, 0, 0)),
             pl.BlockSpec((16, 1024), lambda i: (0, 0)),
         ],
         out_specs=[row, row]
@@ -1054,19 +1102,18 @@
         + [row, pl.BlockSpec((n, FF), lambda i: (i, 0)), fixed(1024), tall]
         + small,
         out_shape=[jax.ShapeDtypeStruct((LOC, D), BF)] * 2
-        + [jax.ShapeDtypeStruct((1, 256), F32)] * 4
+        + [jax.ShapeDtypeStruct((256,), F32)] * 4
         + [
             jax.ShapeDtypeStruct((256, 3 * D), F32),
-            jax.ShapeDtypeStruct((1, 768), F32),
+            jax.ShapeDtypeStruct((768,), F32),
             jax.ShapeDtypeStruct((256, D), F32),
             jax.ShapeDtypeStruct((256, FF), F32),
-            jax.ShapeDtypeStruct((1, 1024), F32),
+            jax.ShapeDtypeStruct((1024,), F32),
             jax.ShapeDtypeStruct((1024, D), F32),
-            jax.ShapeDtypeStruct((1, 256), F32),
+            jax.ShapeDtypeStruct((256,), F32),
         ],
     )(*res)
-    shapes = [(1, LOC, D)] * 2 + [(256,)] * 4 + [None, (768,), None, None, (1024,), None, (256,)]
-    return tuple(a if s is None else a.reshape(s) for a, s in zip(final, shapes))
+    return tuple(a.reshape(1, LOC, D) for a in final[:2]) + tuple(final[2:])
 
 
 def solution(mesh):

time: 208 us -> 176 us (0.85); the launches traced: 205 us -> 176 us
  Pallas kernels: 193 us -> 175 us
  local copies, waits for them, and re-layouts: 5.92 us -> 0 us
  other arithmetic: 5.47 us -> 0 us
    pallas_call x1, Pallas kernels: 183 us -> 166 us  [shards(): pl.pallas_call(body, out_shape=[jax.ShapeDtypeStruct((LOC, D), BF), jax.S...]
    reshape x8 -> x0, local copies, waits for them, and re-layouts: 4.68 us -> none  [shards(): v.reshape(-1, 256)]
where the time goes in v3:
time: 176 us
  Pallas kernels  175 us (99%)
    pallas_call x1, Pallas kernels, shards(): pl.pallas_call(body, out_shape=[jax.ShapeDtypeStruct((LOC, D), BF), jax.S...  166 us
    pallas_call x1, Pallas kernels, shards(): pl.pallas_call(tail, grid=(steps,), in_specs=[row, row, pl.BlockSpec((Z,...  8.57 us

profile of v3, /device:TPU:0, one launch (start us, length us, event | category | flops | bytes accessed | tf_op | source)
XLA Modules:
  0.0 175.6 jit_solution(14734366023497023110)
XLA Ops:
  0.7 166.2 %shard_map.237 = (bf16[256,1024]{1,0:T(8,128)(2,1)}, bf16[256,1024]{1,0:T(8,128)(2,1)}, bf16[4,256,768]{2,1,0:T(8,128)(2,1)}, bf16[4,256,1024]{2,1,0:T(8,128)(2,...) custom-call(bf16[256,1024]{1,0:T(8,128)(2,1)} %bitcast.4, bf16[256,1024]{1,0:T(8,128)(2,1)} %bitcast.5, ...), custom_call_target="tpu_custom_call" | custom-call | tf_op jit(solution)/shard_map/pallas_call | solution.py:1044
  166.9 8.6 %shard_map.238 = (bf16[256,1024]{1,0:T(8,128)(2,1)}, bf16[256,1024]{1,0:T(8,128)(2,1)}, f32[256]{0:T(256)}, f32[256]{0:T(256)}, f32[256]{0:T(256)}, /*index=5*/f...) custom-call(bf16[256,1024]{1,0:T(8,128)(2,1)} %get-tuple-element.32., ...), custom_call_target="tpu_custom_call" | custom-call | tf_op jit(solution)/shard_map/pallas_call | solution.py:1087

commit v4 on v3

--- a/solution.py
+++ b/solution.py
@@ -259,9 +259,10 @@
         def rows(self, c, k):
             return self.buf.at[rows_at(c * LOC + k * piece, piece)]
 
-        def send(self):
+        def send(self, ways=(0, 1, 2)):
+            every = ((mid, ends), (end, middle), (other, middle))
             for k in range(SUB):
-                for dev, when in ((mid, ends), (end, middle), (other, middle)):
+                for dev, when in [every[w] for w in ways]:
                     go(
                         self.src.at[pl.ds(k * piece, piece)],
                         self.rows(z, k),
@@ -795,6 +796,7 @@
         if k == 1:
             gx.hand(c1, other)
             gx.hand(c2, end)
+            gg.send((0,))
         if k == nb - 1:
             gx.wait(c1)
             norm_rows(c1)
@@ -803,32 +805,42 @@
     for copy in own_qkv:
         copy.wait()
     gx.hand(c3, end)
+    gg.send((2,))
     project(z)
     project(c1)
     gx.wait(c2)
     norm_rows(c2)
     project(c2)
+    for copy in w_own:
+        copy.wait()
+
+    @pl.when(z != 2)
+    def _():
+        attend(z)
+
     gx.wait(c3)
-    gg.send()
+    gg.send((1,))
     norm_rows(c3)
     project(c3)
-    for copy in w_own:
-        copy.wait()
+    gg.hand(c1, other)
+    gg.hand(c2, end)
     attend(c3)
     mix(c3)
     attend(c2)
     mix(c2)
-    gg.hand(c1, other)
-    gg.hand(c2, end)
     attend(c1)
     mix(c1)
-    attend(z)
+    gg.hand(c3, end)
+
+    @pl.when(z == 2)
+    def _():
+        attend(z)
+
     mix(z)
     og_own.wait()
     side(z)
     gg.wait(c1)
     side(c1)
-    gg.hand(c3, end)
     attend_back(z)
     attend_back(c1)
     s_out.pass_far(middle)

time: 176 us -> 172 us (0.977)
  Pallas kernels: 175 us -> 171 us
    pallas_call x1, Pallas kernels: 166 us -> 163 us  [shards(): pl.pallas_call(body, out_shape=[jax.ShapeDtypeStruct((LOC, D), BF), jax.S...]
where the time goes in v4:
time: 172 us
  Pallas kernels  171 us (99%)
    pallas_call x1, Pallas kernels, shards(): pl.pallas_call(body, out_shape=[jax.ShapeDtypeStruct((LOC, D), BF), jax.S...  163 us
    pallas_call x1, Pallas kernels, shards(): pl.pallas_call(tail, grid=(steps,), in_specs=[row, row, pl.BlockSpec((Z,...  8.57 us

profile of v4, /device:TPU:0, one launch (start us, length us, event | category | flops | bytes accessed | tf_op | source)
XLA Modules:
  0.0 172.2 jit_solution(5569835937013725043)
XLA Ops:
  0.7 162.8 %shard_map.237 = (bf16[256,1024]{1,0:T(8,128)(2,1)}, bf16[256,1024]{1,0:T(8,128)(2,1)}, bf16[4,256,768]{2,1,0:T(8,128)(2,1)}, bf16[4,256,1024]{2,1,0:T(8,128)(2,...) custom-call(bf16[256,1024]{1,0:T(8,128)(2,1)} %bitcast.4, bf16[256,1024]{1,0:T(8,128)(2,1)} %bitcast.5, ...), custom_call_target="tpu_custom_call" | custom-call | tf_op jit(solution)/shard_map/pallas_call | solution.py:1056
  163.5 8.6 %shard_map.238 = (bf16[256,1024]{1,0:T(8,128)(2,1)}, bf16[256,1024]{1,0:T(8,128)(2,1)}, f32[256]{0:T(256)}, f32[256]{0:T(256)}, f32[256]{0:T(256)}, /*index=5*/f...) custom-call(bf16[256,1024]{1,0:T(8,128)(2,1)} %get-tuple-element.32., ...), custom_call_target="tpu_custom_call" | custom-call | tf_op jit(solution)/shard_map/pallas_call | solution.py:1099

commit v5 on v4

--- a/solution.py
+++ b/solution.py
@@ -547,7 +547,7 @@
             dgelu[at, :] = g
             return carry + g.astype(F32)
 
-        total = lax.fori_loop(0, LOC // 16, act, jnp.zeros((16, 1024), F32))
+        total = lax.fori_loop(0, LOC // 16, act, jnp.zeros((16, 1024), F32), unroll=2)
         vsum[pl.ds(7 + z, 1), :] += jnp.sum(total, axis=0, keepdims=True)
 
     dhid = dgelu
@@ -604,7 +604,7 @@
                 part_i[at, :] = g.astype(BF)
             return carry
 
-        lax.fori_loop(0, LOC // 16, step, 0)
+        lax.fori_loop(0, LOC // 16, step, 0, unroll=2)
 
     def through(sums, weight):
         parts, rest = [], sums

time: 172 us -> 171 us (level)
  no operation moved by 1% of the time
where the time goes in v5:
time: 171 us
  Pallas kernels  170 us (99%)
    pallas_call x1, Pallas kernels, shards(): pl.pallas_call(body, out_shape=[jax.ShapeDtypeStruct((LOC, D), BF), jax.S...  162 us
    pallas_call x1, Pallas kernels, shards(): pl.pallas_call(tail, grid=(steps,), in_specs=[row, row, pl.BlockSpec((Z,...  8.57 us

profile of v5, /device:TPU:0, one launch (start us, length us, event | category | flops | bytes accessed | tf_op | source)
XLA Modules:
  0.0 171.0 jit_solution(15698976574643574660)
XLA Ops:
  0.7 161.6 %shard_map.237 = (bf16[256,1024]{1,0:T(8,128)(2,1)}, bf16[256,1024]{1,0:T(8,128)(2,1)}, bf16[4,256,768]{2,1,0:T(8,128)(2,1)}, bf16[4,256,1024]{2,1,0:T(8,128)(2,...) custom-call(bf16[256,1024]{1,0:T(8,128)(2,1)} %bitcast.4, bf16[256,1024]{1,0:T(8,128)(2,1)} %bitcast.5, ...), custom_call_target="tpu_custom_call" | custom-call | tf_op jit(solution)/shard_map/pallas_call | solution.py:1056
  162.2 8.6 %shard_map.238 = (bf16[256,1024]{1,0:T(8,128)(2,1)}, bf16[256,1024]{1,0:T(8,128)(2,1)}, f32[256]{0:T(256)}, f32[256]{0:T(256)}, f32[256]{0:T(256)}, /*index=5*/f...) custom-call(bf16[256,1024]{1,0:T(8,128)(2,1)} %get-tuple-element.32., ...), custom_call_target="tpu_custom_call" | custom-call | tf_op jit(solution)/shard_map/pallas_call | solution.py:1099
